TPU v7x, 256 devices: a whole 4x4x8 slice. The times are simulated.
256 devices in a mesh: tile: 32 (over x_lo, z, core), win: 8 (over y, x_hi).
Axes of the slice: x: 4 (x_hi: 2, x_lo: 2; x = x_hi * 2 + x_lo), y: 4, z: 8, core: 2. Of those that a mesh axis runs over, the one named last changes fastest.
Arguments:
- spectra: float32 [4, 128, 2, 4096], P(None, 'win', None, 'tile'), may hold values from -6 to 6
- sensor_positions: float32 [2, 4096], replicated, may hold values from -600 to 600
- wavenumbers: float32 [4], replicated, may hold values from 0.02 to 0.2
- sensor_order: int32 [4096], replicated, may hold values from 0 to 4095, each once
- candidates: int32 [4, 1024], replicated, may hold values from 0 to 4095
Outputs:
- csd: float32 [4, 2, 4096, 4096], P(None, None, 'tile', 'win')
- beam: float32 [4, 1024], P(None, ('tile', 'win'))
Inputs may be any that keep to these rules, and one draw needn't show every extreme that they name: `sensor_order`: each acquisition index appears exactly once.
All inputs are finite; a program needn't handle non-finite values.
Results may differ from a plain program's by a relative error of at most 0.0002.
Values sent between devices are 32-bit elements; how exact they have to be, the bound alone decides.
No kernel may reach another device: no remote copies, remote signals or barrier semaphores. Data moves between devices by JAX's collectives and lax.ppermute only.
A program may use at most 128 MiB of HBM per device.

v0:
```python
import jax
import jax.numpy as jnp
from jax import lax
from jax.sharding import PartitionSpec as P

GRID_SIDE = 64


def replica(pos_x, pos_y, cand, wave):
    cand_x = ((cand % GRID_SIDE).astype(jnp.float32) - GRID_SIDE / 2) * 8.0
    cand_z = 50.0 + (cand // GRID_SIDE).astype(jnp.float32) * 4.0
    delta = pos_x[:, None] - cand_x[None, :]
    radius = jnp.sqrt(delta * delta + (pos_y * pos_y)[:, None] + (cand_z * cand_z)[None, :])
    amplitude = 1.0 / radius
    phase = wave * radius
    return (amplitude * jnp.cos(phase), -amplitude * jnp.sin(phase), amplitude)


def cross_density(left_side, right_side):
    hp = lax.Precision.HIGHEST
    left_re = left_side[:, :, 0]
    left_im = left_side[:, :, 1]
    right_re = right_side[:, :, 0]
    right_im = right_side[:, :, 1]
    dens_re = jnp.einsum("fwi,fwj->fij", left_re, right_re, precision=hp) + jnp.einsum(
        "fwi,fwj->fij", left_im, right_im, precision=hp
    )
    dens_im = jnp.einsum("fwi,fwj->fij", left_im, right_re, precision=hp) - jnp.einsum(
        "fwi,fwj->fij", left_re, right_im, precision=hp
    )
    return jnp.stack([dens_re, dens_im], axis=1)


def local(spectra, sensor_positions, wavenumbers, sensor_order, candidates):
    hp = lax.Precision.HIGHEST
    tile_count = lax.axis_size("tile")
    block_count = lax.axis_size("win")
    sensor_total = sensor_order.shape[0]
    row_count = sensor_total // tile_count
    col_count = sensor_total // block_count
    row_start = lax.axis_index("tile") * row_count
    col_start = lax.axis_index("win") * col_count
    total = spectra.shape[1] * block_count
    gathered = lax.all_gather(spectra, "tile", axis=3, tiled=True)
    ordered = jnp.take(gathered, sensor_order, axis=3)
    row_block = lax.dynamic_slice_in_dim(ordered, row_start, row_count, 3)
    all_rows = lax.all_gather(row_block, "win", axis=1, tiled=True)
    all_cols = lax.all_to_all(ordered, "win", split_axis=3, concat_axis=1, tiled=True)
    density = cross_density(all_rows, all_cols) / total
    make_replicas = jax.vmap(replica, in_axes=(None, None, 0, 0))
    row_ids = lax.dynamic_slice_in_dim(sensor_order, row_start, row_count)
    col_ids = lax.dynamic_slice_in_dim(sensor_order, col_start, col_count)
    row_re, row_im, row_amp = make_replicas(
        jnp.take(sensor_positions[0], row_ids),
        jnp.take(sensor_positions[1], row_ids),
        candidates,
        wavenumbers,
    )
    col_re, col_im, col_amp = make_replicas(
        jnp.take(sensor_positions[0], col_ids),
        jnp.take(sensor_positions[1], col_ids),
        candidates,
        wavenumbers,
    )
    dens_re = density[:, 0]
    dens_im = density[:, 1]
    image_re = jnp.einsum("fij,fjc->fic", dens_re, col_re, precision=hp) - jnp.einsum(
        "fij,fjc->fic", dens_im, col_im, precision=hp
    )
    image_im = jnp.einsum("fij,fjc->fic", dens_re, col_im, precision=hp) + jnp.einsum(
        "fij,fjc->fic", dens_im, col_re, precision=hp
    )
    term = jnp.sum(row_re * image_re + row_im * image_im, axis=1)
    share = lax.psum_scatter(term, ("tile", "win"), scatter_dimension=1, tiled=True)
    owned_count = share.shape[1]
    owned = lax.dynamic_slice_in_dim(
        candidates, lax.axis_index(("tile", "win")) * owned_count, owned_count, 1
    )
    own_re, own_im, own_amp = make_replicas(
        sensor_positions[0], sensor_positions[1], owned, wavenumbers
    )
    norm = jnp.sum(own_amp * own_amp, axis=1)
    beam = share / norm
    return (density, beam)


def solution(mesh):
    in_specs = (P(None, "win", None, "tile"), P(), P(), P(), P())
    out_specs = (P(None, None, "tile", "win"), P(None, ("tile", "win")))
    return jax.shard_map(local, mesh=mesh, in_specs=in_specs, out_specs=out_specs, check_vma=False)
```

profile of v0, /device:TPU:1, one launch (start us, length us, event | category | flops | bytes accessed | tf_op | source)
XLA Modules:
  0.0 528.7 jit_solution(2766745406757134554)
XLA Ops:
  7.2 1.8 copy.19
  9.1 0.8 compare_select_fusion.1
  9.9 0.9 fusion.36
  10.7 3.1 gather_fusion.3
  13.9 3.1 gather_fusion.4
  17.0 0.8 compare_select_fusion.2
  17.8 1.1 gather_fusion.1
  19.0 1.1 gather_fusion.2
  20.1 0.8 fusion.25
  22.0 0.8 broadcast_select_fusion.1
  24.9 33.2 %sine_multiply_fusion.8 = f32[4,512,1024]{2,1,0:T(8,128)} fusion(f32[4]{0:T(128)} %param.11, f32[4,1024]{1,0:T(4,128)S(1)} %get-tuple-element.19, f32[512]{0:T(512)S(1)} %select_multiply_fusion, f32[4,1024]{1,0:T(4,128)S(1)} %get-tuple-element.18, f32[512]{0:T(512)S(1)} %get-tuple-element.12), kind=kLoop, calls=%fused_computation.6.clone.1.clone.clone.clone.2 | loop fusion | flops 16777216 | bytes 8425488 | tf_op jit(solution)/shard_map/fij,fjc->fic/dot_general | solution.py:67
  58.1 56.3 %all-gather.2.cloned.1.call-done = f32[4,16,2,4096]{1,0,3,2:T(4,128)} async-done(((f32[4,16,2,128]{1,0,3,2:T(4,128)}), f32[4,16,2,4096]{1,0,3,2:T(4,128)}) %all-gather.2.cloned.1.call-update) | async-done | bytes 2097168 | tf_op jit(solution)/shard_map/all_gather | solution.py:44
  114.4 44.4 %gather_fusion = f32[4096,4,16,2]{2,1,3,0:T(4,128)} fusion(f32[4,16,2,4096]{1,0,3,2:T(4,128)} %all-gather.2.cloned.1.call-done, s32[4096]{0:T(1024)S(1)} %fusion.22), kind=kCustom, calls=%fused_computation.4 | custom fusion | bytes 4210688 | tf_op jit(solution)/shard_map/jit(_take)/gather | solution.py:45
  158.8 16.6 %bitcast_bitcast_fusion = f32[4096,2,4,16]{3,2,1,0:T(4,128)} fusion(f32[4096,4,16,2]{2,1,3,0:T(4,128)} %gather_fusion, pred[4096]{0:T(1024)(128)(4,1)S(1)} %compare_and_fusion), kind=kLoop, calls=%fused_computation.83 | loop fusion | flops 524288 | bytes 4198400
  175.4 15.4 %reshape.89 = f32[8,1,65536]{2,1,0:T(1,128)} reshape(f32[4096,2,4,16]{3,2,1,0:T(4,128)} %bitcast_bitcast_fusion) | data formatting | bytes 4194304
  190.8 6.4 %all-to-all-start = ((f32[8,1,65536]{2,1,0:T(1,128)}), f32[8,1,65536]{2,1,0:T(1,128)S(1)}, u32[]{:S(2)}, u32[]{:S(2)}) async-start(f32[8,1,65536]{2,1,0:T(1,128)} %reshape.89), calls=%async_computation | async-start | bytes 4194304 | tf_op jit(solution)/shard_map/all_to_all | solution.py:48
  197.2 16.2 %broadcast_select_fusion = f32[4096,4,16,2]{2,1,3,0:T(4,128)S(1)} fusion(f32[4096,4,16,2]{2,1,3,0:T(4,128)} %gather_fusion, pred[4096]{0:T(1024)(128)(4,1)S(1)} %compare_and_fusion), kind=kLoop, calls=%fused_computation.5 | loop fusion | flops 524288 | bytes 4198400 | tf_op jit(solution)/shard_map/jit(_take)/select_n | solution.py:45
  213.7 34.9 %all_gather.7 = f32[4,128,2,128]{3,0,2,1:T(4,128)S(1)} all-gather(f32[4,16,2,128]{3,0,2,1:T(4,128)S(1)} %copy.20), channel_id=1, replica_groups=mesh['tile'=32,'win'=8] {'win'}, dimensions={1}, use_global_device_ids=true | all-gather | bytes 589824 | tf_op jit(solution)/shard_map/all_gather | solution.py:47
  248.9 1.3 copy-done
  250.8 7.2 %reduce = f32[8,65536]{1,0:T(8,128)S(1)} reduce(f32[8,1,65536]{2,1,0:T(1,128)} %copy-done, f32[]{:T(128)} %broadcast.137), dimensions={1}, to_apply=%all_to_all.13.reduce_sub_computation | reduce | bytes 4194308 | tf_op jit(solution)/shard_map/all_to_all | solution.py:48
  258.0 17.5 %reshape.90 = f32[4096,2,4,16]{3,2,1,0:T(4,128)} reshape(f32[8,65536]{1,0:T(8,128)S(1)} %reduce) | data formatting | bytes 4194304
  275.5 13.1 %copy.22 = f32[4,16,2,8,512]{4,1,3,0,2:T(8,128)S(1)} copy(f32[4,16,2,8,512]{1,0,2,4,3:T(4,128)} %bitcast.56) | data formatting | bytes 4194304 | tf_op jit(solution)/shard_map/all_to_all | solution.py:48
  288.6 1.0 fusion.9
  289.6 1.0 fusion.8
  290.6 1.0 fusion.7
  291.6 1.0 fusion.6
  292.9 35.3 %fusion.2 = f32[4,128,1024]{2,1,0:T(8,128)S(1)} fusion(f32[4]{0:T(128)S(1)} %copy-done.1, f32[4,1024]{1,0:T(4,128)S(1)} %get-tuple-element.19, f32[512]{0:T(512)S(1)} %select_multiply_fusion, f32[4,1024]{1,0:T(4,128)S(1)} %get-tuple-element.18, f32[512]{0:T(512)S(1)} %get-tuple-element.12, f32[4,2,128,512]{3,2,0,1:T(8,128)S(1)} %maximum_multiply_fusion), kind=kOutput, calls=%fused_computation.11 | convolution fusion | flops 3235905536 | bytes 3183104 | tf_op jit(solution)/shard_map/fij,fjc->fic/dot_general | solution.py:70
  328.2 47.9 %fusion.3 = f32[4,128,1024]{2,1,0:T(8,128)S(1)} fusion(f32[4]{0:T(128)S(1)} %copy-done.1, f32[4,1024]{1,0:T(4,128)S(1)} %get-tuple-element.19, f32[512]{0:T(512)S(1)} %select_multiply_fusion, f32[4,1024]{1,0:T(4,128)S(1)} %get-tuple-element.18, f32[512]{0:T(512)S(1)} %get-tuple-element.12, f32[4,2,128,512]{3,2,0,1:T(8,128)S(1)} %maximum_multiply_fusion), kind=kOutput, calls=%fused_computation.12 | convolution fusion | flops 3235905536 | bytes 3183104 | tf_op jit(solution)/shard_map/fij,fjc->fic/dot_general | solution.py:67
  376.1 48.8 %fusion.4 = f32[4,128,1024]{2,1,0:T(8,128)S(1)} fusion(f32[4]{0:T(128)S(1)} %copy-done.1, f32[4,1024]{1,0:T(4,128)S(1)} %get-tuple-element.19, f32[512]{0:T(512)S(1)} %select_multiply_fusion, f32[4,1024]{1,0:T(4,128)S(1)} %get-tuple-element.18, f32[512]{0:T(512)S(1)} %get-tuple-element.12, f32[4,2,128,512]{3,2,0,1:T(8,128)S(1)} %maximum_multiply_fusion), kind=kOutput, calls=%fused_computation.13 | convolution fusion | flops 3238002688 | bytes 3183104 | tf_op jit(solution)/shard_map/fij,fjc->fic/dot_general | solution.py:70
  424.9 1.6 copy.24
  426.5 14.1 %add_reduce_fusion = f32[4,1024]{1,0:T(4,128)S(1)} fusion(f32[4,128,1024]{2,1,0:T(8,128)S(1)} %fusion.4, f32[4,128,1024]{2,1,0:T(8,128)S(1)} %fusion.2, f32[4,128,1024]{2,1,0:T(8,128)S(1)} %fusion.3, f32[4]{0:T(128)S(1)} %copy-done.1, f32[4,1024]{1,0:T(4,128)S(1)} %get-tuple-element.19, f32[4,1024]{1,0:T(4,128)S(1)} %get-tuple-element.18, ...), kind=kOutput, calls=%fused_computation.16 | convolution fusion | flops 3229085696 | bytes 15779328 | tf_op jit(solution)/shard_map/fij,fjc->fic/dot_general | solution.py:67
  440.6 80.4 %all-reduce = f32[4,1024]{1,0:T(4,128)S(1)} all-reduce(f32[4,1024]{1,0:T(4,128)S(1)} %add_reduce_fusion), channel_id=2, replica_groups=mesh['tile'=32,'win'=8] {'tile','win'}, use_global_device_ids=true, to_apply=%region_1.4.clone | all-reduce | flops 4096 | bytes 32768
  (28 shorter events, 5.4 us)
Async XLA Ops:
  7.2 107.3 %all-gather.2.cloned.1.call-start = ((), (), s32[]{:S(2)}) async-start(), calls=%async_computation.1 | async-start | bytes 17301504 | tf_op jit(solution)/shard_map/all_gather | solution.py:44
  190.8 58.2 %all-to-all-start = ((f32[8,1,65536]{2,1,0:T(1,128)}), f32[8,1,65536]{2,1,0:T(1,128)S(1)}, u32[]{:S(2)}, u32[]{:S(2)}) async-start(f32[8,1,65536]{2,1,0:T(1,128)} %reshape.89), calls=%async_computation | async-start | bytes 4194304 | tf_op jit(solution)/shard_map/all_to_all | solution.py:48
  248.9 1.3 copy-start
  288.6 4.3 copy-start.1
  328.2 98.3 %slice-start = ((s8[8388608]{0:T(1024)(128)(4,1)}), s8[4194304]{0:T(1024)(128)(4,1)S(1)}, s32[]{:S(2)}) async-start(s8[8388608]{0:T(1024)(128)(4,1)} %bitcast.61), calls=%async_computation.2 | async-start | bytes 8388608
  376.1 50.4 %slice-start.1 = ((s8[8388608]{0:T(1024)(128)(4,1)}), s8[4194304]{0:T(1024)(128)(4,1)S(1)}, s32[]{:S(2)}) async-start(s8[8388608]{0:T(1024)(128)(4,1)} %bitcast.61), calls=%async_computation.3 | async-start | bytes 8388608
Sparse Core Ops, SparseCore 0:
  10.4 103.9 all-gather.1
where the time goes:
time: 537 us; the launch traced here: 529 us
  matrix products  150 us (28%)
  blocking collectives  115 us (21%)
  local copies, waits for them, and re-layouts  106 us (20%)
  other arithmetic  80.4 us (15%)
  waiting for transfers between devices  56.4 us (11%)
  between operations  14.5 us (3%)
  starting transfers between devices  6.46 us (1%)
    unnamed x1, blocking collectives  80.4 us
    all_gather x1, waiting for transfers between devices, local(): gathered = lax.all_gather(spectra, 'tile', axis=3, tiled=True)  56.3 us
    dot_general x1, matrix products, local(): jnp.einsum('fij,fjc->fic', dens_re, col_im, precision=hp)  48.8 us
    dot_general x1, matrix products, local(): jnp.einsum('fij,fjc->fic', dens_re, col_re, precision=hp)  47.9 us
    gather x1, local copies, waits for them, and re-layouts, local(): ordered = jnp.take(gathered, sensor_order, axis=3)  44.4 us
    unnamed x14, local copies, waits for them, and re-layouts  37.9 us
    dot_general x1, matrix products, local(): jnp.einsum('fij,fjc->fic', dens_im, col_re, precision=hp)  35.3 us
    all_gather x1, blocking collectives, local(): all_rows = lax.all_gather(row_block, 'win', axis=1, tiled=True)  34.9 us
  transfers between devices with their start and end apart: 2, of which 1 were waited for; matrix products, arithmetic and copies ran while one was open for 12% of the time, Pallas kernels for 0%

commit v1 on v0

v1 whole, which is shorter than its diff:
```python
import jax
import jax.numpy as jnp
import numpy as np
from jax import lax
from jax.experimental import pallas as pl
from jax.experimental.pallas import tpu as pltpu
from jax.sharding import Mesh, PartitionSpec as P

GRID_SIDE = 64
SENSORS = 4096
WINDOWS = 128
LANES = 128
SEGS = SENSORS // LANES
ROWS = 32
DESTS = 32
CANDS = 128
MSG = 3 * ROWS + 8
TILE = ("xl", "z", "core")
PLANE = ("xl", "core", "y", "xh")


def turn_series():
    x = np.cos(np.linspace(0.0, np.pi, 4001)) * 0.5
    y = x * x
    powers = y[:, None] ** np.arange(8)[None, :]
    cos_c = np.linalg.lstsq(powers, np.cos(2 * np.pi * x), rcond=None)[0]
    sinc = 2 * np.pi * np.sinc(2 * x)
    sin_c = np.linalg.lstsq(powers, sinc, rcond=None)[0]
    return [float(v) for v in cos_c], [float(v) for v in sin_c]


COS_C, SIN_C = turn_series()


def split(value):
    high = value.astype(jnp.bfloat16)
    low = (value - high.astype(jnp.float32)).astype(jnp.bfloat16)
    return high, low


def swap_pairs(value):
    count = value.shape[0]
    up = pltpu.roll(value, count - 1, 0)
    down = pltpu.roll(value, 1, 0)
    row = lax.broadcasted_iota(jnp.int32, value.shape, 0)
    return jnp.where(row % 2 == 0, up, -down)


def replica_kernel(turn_ref, pos_ref, cx_ref, cz_ref, high_ref, low_ref, scale_ref, acc):
    turn = turn_ref[0]
    acc[...] = jnp.zeros_like(acc)

    @pl.loop(0, SEGS // 2)
    def _(pair):
        for half in range(2):
            seg = pair * 2 + half
            px = pos_ref[0, pl.ds(seg, 1), :]
            py = pos_ref[1, pl.ds(seg, 1), :]
            py2 = py * py
            for part in range(CANDS // 32):
                own = slice(part * 32, part * 32 + 32)
                delta = px - cx_ref[own, :]
                cz = cz_ref[own, :]
                r2 = delta * delta + py2 + cz * cz
                inv = lax.rsqrt(r2)
                turns = (r2 * inv) * turn
                x = turns - jnp.round(turns)
                y = x * x
                cos = jnp.full_like(y, COS_C[7])
                sin = jnp.full_like(y, SIN_C[7])
                for power in range(6, -1, -1):
                    cos = cos * y + COS_C[power]
                    sin = sin * y + SIN_C[power]
                re_h, re_l = split(inv * cos)
                im_h, im_l = split(-(inv * x) * sin)
                lanes = slice(half * LANES, half * LANES + LANES)
                own_im = slice(CANDS + part * 32, CANDS + part * 32 + 32)
                high_ref[pair, own, lanes] = re_h
                low_ref[pair, own, lanes] = re_l
                high_ref[pair, own_im, lanes] = im_h
                low_ref[pair, own_im, lanes] = im_l
                acc[own, :] += inv * inv

    norm = jnp.sum(acc[...].T, axis=0, keepdims=True)
    scale_ref[...] = jnp.broadcast_to(1.0 / (WINDOWS * norm), (8, CANDS))


def make_replicas(turn, positions, cand_x, cand_z):
    full = lambda *s: pl.BlockSpec(memory_space=pltpu.VMEM)
    return pl.pallas_call(
        replica_kernel,
        out_shape=(
            jax.ShapeDtypeStruct((SEGS // 2, 2 * CANDS, 2 * LANES), jnp.bfloat16),
            jax.ShapeDtypeStruct((SEGS // 2, 2 * CANDS, 2 * LANES), jnp.bfloat16),
            jax.ShapeDtypeStruct((8, CANDS), jnp.float32),
        ),
        in_specs=[pl.BlockSpec(memory_space=pltpu.SMEM)] + [full()] * 3,
        out_specs=(full(), full(), full()),
        scratch_shapes=[pltpu.VMEM((CANDS, LANES), jnp.float32)],
        compiler_params=pltpu.CompilerParams(vmem_limit_bytes=32 * 1024 * 1024),
        cost_estimate=pl.CostEstimate(flops=30_000_000, bytes_accessed=5_000_000, transcendentals=600_000),
        name="replicas",
    )(turn, positions, cand_x, cand_z)


def pack_kernel(z_ref, order_ref, spec_ref, high_ref, low_ref, scale_ref, out_ref, held, proj):
    contract = (((1,), (1,)), ((), ()))
    proj[...] = jnp.zeros_like(proj)

    @pl.loop(0, SEGS // 2)
    def _(pair):
        data = jnp.concatenate([spec_ref[pair * 2], spec_ref[pair * 2 + 1]], axis=1)
        data_h, data_l = split(data)
        both = jnp.concatenate([data_h, data_l], axis=0)
        first = lax.dot_general(both, high_ref[pair], contract, preferred_element_type=jnp.float32)
        second = lax.dot_general(data_h, low_ref[pair], contract, preferred_element_type=jnp.float32)
        proj[...] += first[:ROWS] + first[ROWS:] + second
        for half in range(2):
            seg = pair * 2 + half
            index = jnp.broadcast_to(order_ref[pl.ds(seg, 1), :], (ROWS, LANES))
            lane = index % LANES
            home = index // LANES
            total = jnp.zeros((ROWS, LANES), jnp.float32)
            for run in range(SEGS):
                there = jnp.take_along_axis(spec_ref[run], lane, axis=1)
                total = jnp.where(home == run, there, total)
            held[seg] = total

    value = proj[:, :CANDS] + swap_pairs(proj[:, CANDS:])
    power = jnp.sum(value * value, axis=0, keepdims=True) * scale_ref[...]
    z = z_ref[0]
    for xl in range(2):
        for core in range(2):
            mine = held[xl * 16 + z * 2 + core]
            for block in range(8):
                dest = (xl * 2 + core) * 8 + block
                out_ref[dest, 0:ROWS, :] = mine
                for run in range(2):
                    out_ref[dest, (1 + run) * ROWS:(2 + run) * ROWS, :] = held[block * 4 + core * 2 + run]
                out_ref[dest, 3 * ROWS:, :] = power


def make_messages(z, order, spec, high, low, scale):
    full = lambda: pl.BlockSpec(memory_space=pltpu.VMEM)
    return pl.pallas_call(
        pack_kernel,
        out_shape=jax.ShapeDtypeStruct((DESTS, MSG, LANES), jnp.float32),
        in_specs=[pl.BlockSpec(memory_space=pltpu.SMEM)] + [full()] * 5,
        out_specs=full(),
        scratch_shapes=[
            pltpu.VMEM((SEGS, ROWS, LANES), jnp.float32),
            pltpu.VMEM((ROWS, 2 * CANDS), jnp.float32),
        ],
        compiler_params=pltpu.CompilerParams(vmem_limit_bytes=32 * 1024 * 1024),
        cost_estimate=pl.CostEstimate(flops=200_000_000, bytes_accessed=6_000_000, transcendentals=0),
        name="messages",
    )(z, order, spec, high, low, scale)


def density_kernel(core_ref, own_ref, other_ref, out_ref):
    depth = 8 * ROWS
    rows = own_ref[0, :, 0:ROWS, :].reshape(depth, LANES) * (1.0 / WINDOWS)
    left = jnp.concatenate([rows, swap_pairs(rows)], axis=1)
    left_h, left_l = split(left.T)
    contract = (((1,), (0,)), ((), ()))
    core = core_ref[0]
    for half, source, base in ((core, own_ref, ROWS), (1 - core, other_ref, 0)):
        parts = [source[0, :, base + run * ROWS:base + (run + 1) * ROWS, :].reshape(depth, LANES) for run in range(2)]
        right_h, right_l = split(jnp.concatenate(parts, axis=1))
        total = lax.dot_general(left_h, right_h, contract, preferred_element_type=jnp.float32)
        total += lax.dot_general(left_h, right_l, contract, preferred_element_type=jnp.float32)
        total += lax.dot_general(left_l, right_h, contract, preferred_element_type=jnp.float32)
        place = pl.ds(pl.multiple_of(half * 2 * LANES, 2 * LANES), 2 * LANES)
        out_ref[0, 0, :, place] = total[:LANES]
        out_ref[0, 1, :, place] = total[LANES:]


def make_density(core, own, other):
    freqs = own.shape[0]
    return pl.pallas_call(
        density_kernel,
        grid=(freqs,),
        out_shape=jax.ShapeDtypeStruct((freqs, 2, LANES, 4 * LANES), jnp.float32),
        in_specs=[
            pl.BlockSpec(memory_space=pltpu.SMEM),
            pl.BlockSpec((1, 8, MSG, LANES), lambda f: (f, 0, 0, 0)),
            pl.BlockSpec((1, 8, 2 * ROWS, LANES), lambda f: (f, 0, 0, 0)),
        ],
        out_specs=pl.BlockSpec((1, 2, LANES, 4 * LANES), lambda f: (f, 0, 0, 0)),
        compiler_params=pltpu.CompilerParams(vmem_limit_bytes=32 * 1024 * 1024),
        name="density",
    )(core, own, other)


def local(spectra, sensor_positions, wavenumbers, sensor_order, candidates):
    xl, z, core = (lax.axis_index(name) for name in TILE)
    freq = xl * 2 + core
    outgoing = jnp.broadcast_to(spectra.reshape(2, 1, 2, ROWS, LANES), (2, 8, 2, ROWS, LANES))
    gathered = lax.all_to_all(outgoing.reshape(DESTS, ROWS, LANES), TILE, 0, 0, tiled=True)
    grid = lax.dynamic_index_in_dim(candidates, freq, 0, keepdims=False)
    grid = lax.dynamic_index_in_dim(grid.reshape(2, 8, 2, 32), z, 1, keepdims=False).reshape(CANDS, 1)
    cand_x = ((grid % GRID_SIDE).astype(jnp.float32) - GRID_SIDE / 2) * 8.0
    cand_z = 50.0 + (grid // GRID_SIDE).astype(jnp.float32) * 4.0
    turn = lax.dynamic_slice_in_dim(wavenumbers, freq, 1) * (0.5 / np.pi)
    high, low, scale = make_replicas(
        turn.astype(jnp.float32),
        sensor_positions.reshape(2, SEGS, LANES),
        jnp.broadcast_to(cand_x, (CANDS, LANES)),
        jnp.broadcast_to(cand_z, (CANDS, LANES)),
    )
    messages = make_messages(z.reshape(1), sensor_order.reshape(SEGS, LANES), gathered, high, low, scale)
    received = lax.all_to_all(messages, PLANE, 0, 0, tiled=True).reshape(4, 8, MSG, LANES)
    columns = received[:, :, ROWS:3 * ROWS, :]
    other = lax.ppermute(columns, "core", [(0, 1), (1, 0)])
    density = make_density(core.reshape(1), received, other)
    shares = jnp.sum(received[:, :, 3 * ROWS, :], axis=1)
    mine = lax.axis_index(PLANE) * 4
    beam = lax.dynamic_slice_in_dim(shares, mine, 4, 1)
    return (density, beam)


def solution(mesh):
    fine = Mesh(mesh.devices.reshape(2, 8, 2, 4, 2), ("xl", "z", "core", "y", "xh"))
    in_specs = (P(None, ("y", "xh"), None, TILE), P(), P(), P(), P())
    out_specs = (P(None, None, TILE, ("y", "xh")), P(None, TILE + ("y", "xh")))
    return jax.shard_map(local, mesh=fine, in_specs=in_specs, out_specs=out_specs, check_vma=False)
```

time: 537 us -> 78 us (0.15); the launches traced: 529 us -> 77.6 us
  matrix products: 150 us -> 0 us
  local copies, waits for them, and re-layouts: 106 us -> 8.73 us
  blocking collectives: 115 us -> 33.1 us
  other arithmetic: 80.4 us -> 0.04 us
  waiting for transfers between devices: 56.4 us -> 9.99 us
  between operations: 14.5 us -> 1.37 us
  Pallas kernels: 0 us -> 12.9 us
    dot_general x8 -> x0, matrix products: 150 us -> none  [the longest x1 48.8 us: local(): jnp.einsum('fij,fjc->fic', dens_re, col_im, precision=hp)]
    unnamed x1 -> x0, blocking collectives: 80.4 us -> none
    all_gather x1 -> x0, waiting for transfers between devices: 56.3 us -> none  [local(): gathered = lax.all_gather(spectra, 'tile', axis=3, tiled=True)]
    gather x5 -> x0, local copies, waits for them, and re-layouts: 52.9 us -> none  [the longest x1 44.4 us: local(): ordered = jnp.take(gathered, sensor_order, axis=3)]
    all_gather x1 -> x0, blocking collectives: 34.9 us -> none  [local(): all_rows = lax.all_gather(row_block, 'win', axis=1, tiled=True)]
    unnamed x14 -> x9, local copies, waits for them, and re-layouts: 37.9 us -> 3.69 us
    dot_general x1 -> x0, other arithmetic: 33.2 us -> none  [local(): jnp.einsum('fij,fjc->fic', dens_im, col_im, precision=hp)]
    all_to_all x0 -> x1, blocking collectives: none -> 33.1 us  [local(): lax.all_to_all(messages, PLANE, 0, 0, tiled=True).reshape(4, 8, MSG, LANES)]
  transfers between devices with their start and end apart: 2 -> 2, of which waited for: 1 -> 2; matrix products, arithmetic and copies ran while one was open for 12% -> 4% of each run, Pallas kernels for 0% -> 5%
where the time goes in v1:
time: 78 us; the launch traced here: 77.6 us
  blocking collectives  33.1 us (42%)
  Pallas kernels  12.9 us (17%)
  starting transfers between devices  11.5 us (15%)
  waiting for transfers between devices  9.99 us (13%)
  local copies, waits for them, and re-layouts  8.73 us (11%)
  between operations  1.37 us (2%)
    all_to_all x1, blocking collectives, local(): lax.all_to_all(messages, PLANE, 0, 0, tiled=True).reshape(4, 8, MSG, LANES)  33.1 us
    all_to_all x1, starting transfers between devices, local(): lax.all_to_all(outgoing.reshape(DESTS, ROWS, LANES), TILE, 0, 0, tiled=True)  11.1 us
    all_to_all x1, waiting for transfers between devices, local(): lax.all_to_all(outgoing.reshape(DESTS, ROWS, LANES), TILE, 0, 0, tiled=True)  8.17 us
    pallas_call x1, Pallas kernels, make_messages(): pl.pallas_call(pack_kernel, out_shape=jax.ShapeDtypeStruct((DESTS, MSG, L...  5.91 us
    pallas_call x1, Pallas kernels, make_replicas(): pl.pallas_call(replica_kernel, out_shape=(jax.ShapeDtypeStruct((SEGS // 2...  4.01 us
    unnamed x9, local copies, waits for them, and re-layouts  3.69 us
    pallas_call x1, Pallas kernels, make_density(): pl.pallas_call(density_kernel, grid=(freqs,), out_shape=jax.ShapeDtypeStr...  2.98 us
    ppermute x1, waiting for transfers between devices, local(): other = lax.ppermute(columns, 'core', [(0, 1), (1, 0)])  1.82 us
  transfers between devices with their start and end apart: 2, of which 2 were waited for; matrix products, arithmetic and copies ran while one was open for 4% of the time, Pallas kernels for 5%

profile of v1, /device:TPU:1, one launch (start us, length us, event | category | flops | bytes accessed | tf_op | source)
XLA Modules:
  0.0 77.6 jit_solution(7725079551175534548)
XLA Ops:
  0.6 0.0 copy-start
  0.6 0.0 copy-start.3
  0.7 1.7 %broadcast_in_dim.18 = f32[2,8,2,32,128]{4,3,2,1,0:T(8,128)} broadcast(f32[2,2,32,128]{3,2,1,0:T(8,128)} %bitcast.15), dimensions={0,2,3,4} | broadcast | bytes 589824 | tf_op jit(solution)/shard_map/broadcast_in_dim | solution.py:198
  2.4 11.1 %all-to-all-start = ((f32[32,32,128]{2,1,0:T(8,128)}), f32[32,32,128]{2,1,0:T(8,128)S(1)}, u32[]{:S(2)}, u32[]{:S(2)}) async-start(f32[32,32,128]{2,1,0:T(8,128)} %bitcast.4), calls=%async_computation | async-start | bytes 1048576 | tf_op jit(solution)/shard_map/all_to_all | solution.py:199
  13.4 1.2 %dynamic_slice.14 = f32[1]{0:T(128)} dynamic-slice(f32[4]{0:T(128)} %param.7, s32[]{:T(128)S(6)} %select_n.34), dynamic_slice_sizes={1} | dynamic-slice | bytes 12 | tf_op jit(solution)/shard_map/dynamic_slice | solution.py:204
  14.7 0.0 copy-done
  14.7 0.1 reshape.136
  14.8 0.1 reshape.137
  14.9 0.8 copy.9
  16.3 0.1 broadcast_in_dim.20.cz_ref
  16.4 0.1 broadcast_in_dim.19.cx_ref
  16.5 4.0 %replicas.1 = (bf16[16,256,256]{2,1,0:T(8,128)(2,1)S(1)}, bf16[16,256,256]{2,1,0:T(8,128)(2,1)S(1)}, f32[8,128]{1,0:T(8,128)S(1)}) custom-call(f32[1]{0:T(128)S(6)} %mul.41.turn_ref, f32[2,32,128]{2,1,0:T(8,128)S(1)} %bitcast.13, f32[128,128]{1,0:T(8,128)S(1)} %broadcast_in_dim.19.cx_ref, f32[128,128]{1,0:T(8,128)S(1)} %broadcast_in_dim.20.cz_ref), custom_call_target="tpu_custom_call" | custom-call | flops 30000000 | bytes 5000000 | tf_op jit(solution)/shard_map/replicas/pallas_call | solution.py:90
  20.5 0.0 copy-start.1
  20.5 1.3 %copy-done.1 = bf16[16,256,256]{2,1,0:T(8,128)(2,1)} copy-done((bf16[16,256,256]{2,1,0:T(8,128)(2,1)}, bf16[16,256,256]{2,1,0:T(8,128)(2,1)S(1)}, u32[]{:S(2)}) %copy-start.1) | copy-done | bytes 2097176
  21.8 8.2 %all-to-all-done.spec_ref = f32[32,32,128]{2,1,0:T(8,128)S(1)} async-done(((f32[32,32,128]{2,1,0:T(8,128)}), f32[32,32,128]{2,1,0:T(8,128)S(1)}, u32[]{:S(2)}, u32[]{:S(2)}) %all-to-all-start) | async-done | bytes 524320 | tf_op jit(solution)/shard_map/all_to_all | solution.py:199
  30.0 0.0 copy-done.3
  30.0 0.0 copy-start.2
  30.0 1.6 %copy-done.2 = bf16[16,256,256]{2,1,0:T(8,128)(2,1)S(1)} copy-done((bf16[16,256,256]{2,1,0:T(8,128)(2,1)S(1)}, bf16[16,256,256]{2,1,0:T(8,128)(2,1)}, u32[]{:S(2)}) %copy-start.2) | copy-done | bytes 2097176
  31.6 5.9 %messages.1 = f32[32,104,128]{2,1,0:T(8,128)S(1)} custom-call(s32[1]{0:T(128)} %bitcast.1.z_ref, s32[32,128]{1,0:T(8,128)S(1)} %bitcast.14, f32[32,32,128]{2,1,0:T(8,128)S(1)} %all-to-all-done.spec_ref, bf16[16,256,256]{2,1,0:T(8,128)(2,1)S(1)} %get-tuple-element.5.high_ref, bf16[16,256,256]{2,1,0:T(8,128)(2,1)S(1)} %copy-done.2, ...), custom_call_target="tpu_custom_call" | custom-call | flops 200000000 | bytes 6000000 | tf_op jit(solution)/shard_map/messages/pallas_call | solution.py:145
  37.5 33.1 %all_to_all.10 = f32[32,104,128]{2,1,0:T(8,128)S(1)} all-to-all(f32[32,104,128]{2,1,0:T(8,128)S(1)} %messages.1), channel_id=1, replica_groups=mesh['xl'=2,'z'=8,'core'=2,'y'=4,'xh'=2] {'xl','core','y','xh'}, dimensions={0} | all-to-all | bytes 3407872 | tf_op jit(solution)/shard_map/all_to_all | solution.py:212
  70.6 1.1 %slice.8 = f32[4,8,64,128]{3,2,1,0:T(8,128)} slice(f32[4,8,104,128]{3,2,1,0:T(8,128)S(1)} %bitcast.10), slice={[0:4], [0:8], [32:96], [0:128]} | slice | bytes 2097152 | tf_op jit(solution)/shard_map/slice | solution.py:213
  71.7 0.4 collective-permute-start
  72.2 0.7 constant_dynamic-slice_fusion
  72.8 1.8 %collective-permute-done.other_ref = f32[4,8,64,128]{3,2,1,0:T(8,128)S(1)} collective-permute-done((f32[4,8,64,128]{3,2,1,0:T(8,128)}, f32[4,8,64,128]{3,2,1,0:T(8,128)S(1)}, u32[]{:S(2)}, u32[]{:S(2)}) %collective-permute-start) | collective-permute-done | bytes 1048608 | tf_op jit(solution)/shard_map/ppermute | solution.py:214
  74.6 3.0 %density.1 = f32[4,2,128,512]{3,2,1,0:T(8,128)} custom-call(s32[1]{0:T(128)} %bitcast.core_ref, f32[4,8,104,128]{3,2,1,0:T(8,128)S(1)} %bitcast.12, f32[4,8,64,128]{3,2,1,0:T(8,128)S(1)} %collective-permute-done.other_ref), custom_call_target="tpu_custom_call" | custom-call | tf_op jit(solution)/shard_map/density/pallas_call | solution.py:180
  (4 shorter events, 0.1 us)
Async XLA Ops:
  0.6 14.0 %copy-start = (s32[4,1024]{1,0:T(4,128)S(1)}, s32[4,1024]{1,0:T(4,128)}, u32[]{:S(2)}) copy-start(s32[4,1024]{1,0:T(4,128)} %param.9) | copy-start | bytes 49156
  0.6 29.3 %copy-start.3 = (s32[4096]{0:T(1024)S(1)}, s32[4096]{0:T(1024)}, u32[]{:S(2)}) copy-start(s32[4096]{0:T(1024)} %param.8) | copy-start | bytes 49156
  2.4 27.6 %all-to-all-start = ((f32[32,32,128]{2,1,0:T(8,128)}), f32[32,32,128]{2,1,0:T(8,128)S(1)}, u32[]{:S(2)}, u32[]{:S(2)}) async-start(f32[32,32,128]{2,1,0:T(8,128)} %bitcast.4), calls=%async_computation | async-start | bytes 1048576 | tf_op jit(solution)/shard_map/all_to_all | solution.py:199
  20.5 1.3 %copy-start.1 = (bf16[16,256,256]{2,1,0:T(8,128)(2,1)}, bf16[16,256,256]{2,1,0:T(8,128)(2,1)S(1)}, u32[]{:S(2)}) copy-start(bf16[16,256,256]{2,1,0:T(8,128)(2,1)S(1)} %get-tuple-element.6.low_ref) | copy-start | bytes 6291460
  30.0 1.6 %copy-start.2 = (bf16[16,256,256]{2,1,0:T(8,128)(2,1)S(1)}, bf16[16,256,256]{2,1,0:T(8,128)(2,1)}, u32[]{:S(2)}) copy-start(bf16[16,256,256]{2,1,0:T(8,128)(2,1)} %copy-done.1) | copy-start | bytes 6291460
  71.7 2.9 %collective-permute-start = (f32[4,8,64,128]{3,2,1,0:T(8,128)}, f32[4,8,64,128]{3,2,1,0:T(8,128)S(1)}, u32[]{:S(2)}, u32[]{:S(2)}) collective-permute-start(f32[4,8,64,128]{3,2,1,0:T(8,128)} %slice.8), channel_id=1, source_target_pairs={{0,8},{8,0},{1,9},{9,1},{2,10},{10,2},{3,11},{11,3},{4,12},{12,4},... | collective-permute-start | bytes 3145736 | tf_op jit(solution)/shard_map/ppermute | solution.py:214

commit v2 on v0

v2 whole, which is shorter than its diff:
```python
import jax
import jax.numpy as jnp
import numpy as np
from jax import lax
from jax.experimental import pallas as pl
from jax.experimental.pallas import tpu as pltpu
from jax.sharding import Mesh, PartitionSpec as P

GRID_SIDE = 64
WINDOWS = 128
LANES = 128
SEGS = 32
ROWS = 16
PEERS = 64
MSG = 3 * ROWS + 2
VMEM_LIMIT = 24 * 1024 * 1024
NAMES = ("xl", "zh", "zl", "core", "y", "xh")
SIZES = (2, 4, 2, 2, 4, 2)
TILE = ("xl", "zh", "zl", "core")
WIN = ("y", "xh")
GATHER = ("core", "xl", "zh", "zl")
SPREAD = ("y", "xl", "xh", "zl", "core")

PEER = [(y, xl, xh, zl, core) for y in range(4) for xl in range(2) for xh in range(2) for zl in range(2) for core in range(2)]
HOLDERS = [[n for n, p in enumerate(PEER) if p[4] * 2 + p[1] == freq] for freq in range(4)]


def tile_of(run):
    return (run % 16) * 2 + run // 16


def half_turn_series():
    x = np.cos(np.linspace(0.0, np.pi, 4001)) * 0.5
    y = x * x
    powers = y[:, None] ** np.arange(5)[None, :]
    sin_c = np.linalg.lstsq(powers[:, :5], np.sqrt(2.0) * np.pi * np.sinc(x), rcond=None)[0]
    cos_c = np.linalg.lstsq(powers[:, :5], -np.sqrt(2.0) * np.cos(np.pi * x), rcond=None)[0]
    return [float(v) for v in sin_c], [float(v) for v in cos_c]


SIN_C, COS_C = half_turn_series()


def series(coefficients, y):
    total = coefficients[-1] * y + coefficients[-2]
    for c in coefficients[-3::-1]:
        total = total * y + c
    return total


def in_vmem():
    return pl.BlockSpec(memory_space=pltpu.VMEM)


def in_hbm():
    return pl.BlockSpec(memory_space=pltpu.HBM)


def keep_in_hbm(array):
    return pltpu.with_memory_space_constraint(array, pltpu.HBM)


def my_freq():
    return lax.axis_index("core") * 2 + lax.axis_index("xl")


def split(value):
    high = value.astype(jnp.bfloat16)
    low = (value - high.astype(jnp.float32)).astype(jnp.bfloat16)
    return high, low


def swap_pairs(value):
    count = value.shape[0]
    up = pltpu.roll(value, count - 1, 0)
    down = pltpu.roll(value, 1, 0)
    row = lax.broadcasted_iota(jnp.int32, value.shape, 0)
    return jnp.where(row % 2 == 0, up, -down)


def replica_kernel(pos_hbm, cand_hbm, wave_hbm, high_hbm, low_hbm, pos_ref, cand_ref, wave_ref, high_ref, low_ref, sem):
    pairs = ((pos_hbm, pos_ref), (cand_hbm, cand_ref), (wave_hbm, wave_ref))
    loads = [pltpu.make_async_copy(src, dst, sem.at[2 + n]) for n, (src, dst) in enumerate(pairs)]
    for load in loads:
        load.start()
    for load in loads:
        load.wait()
    freq, zh = my_freq(), lax.axis_index("zh")
    turn = wave_ref[freq] * (0.5 / np.pi)
    cx, cz2 = [], []
    for xl in range(2):
        lanes = pl.ds(pl.multiple_of((xl * 4 + zh) * LANES, LANES), LANES)
        grids = cand_ref[:, lanes]
        bin_of = lax.broadcasted_iota(jnp.int32, grids.shape, 0)
        grid = jnp.sum(jnp.where(bin_of == freq, grids, 0), axis=0, keepdims=True)
        cx.append(((grid % GRID_SIDE).astype(jnp.float32) - GRID_SIDE / 2) * 8.0)
        depth = 50.0 + (grid // GRID_SIDE).astype(jnp.float32) * 4.0
        cz2.append(depth * depth)

    def stores(pair):
        return [
            pltpu.make_async_copy(src.at[pair], dst.at[pair], sem.at[n])
            for n, (src, dst) in enumerate(((high_ref, high_hbm), (low_ref, low_hbm)))
        ]

    @pl.loop(0, SEGS // 2)
    def _(pair):
        for half in range(2):
            lanes = pl.ds(pl.multiple_of(tile_of(pair * 2 + half) * LANES, LANES), LANES)
            px = jnp.broadcast_to(pos_ref[0:1, lanes], (LANES, LANES)).T
            py = pos_ref[1:2, lanes]
            py2 = jnp.broadcast_to(py * py, (LANES, LANES)).T
            for xl in range(2):
                for part in range(LANES // 32):
                    own = slice(part * 32, part * 32 + 32)
                    delta = px[own] - cx[xl]
                    r2 = delta * delta + (py2[own] + cz2[xl])
                    inv = lax.rsqrt(r2)
                    turns = (r2 * inv) * turn
                    x = turns - jnp.round(turns)
                    y = x * x
                    sin = x * series(SIN_C, y)
                    most = inv * sin
                    re_h, re_l = split(inv - most * sin)
                    im_h, im_l = split(most * series(COS_C, y))
                    rows = slice(half * LANES + part * 32, half * LANES + part * 32 + 32)
                    re = slice(xl * 2 * LANES, xl * 2 * LANES + LANES)
                    im = slice(xl * 2 * LANES + LANES, xl * 2 * LANES + 2 * LANES)
                    high_ref[pair, rows, re] = re_h
                    low_ref[pair, rows, re] = re_l
                    high_ref[pair, rows, im] = im_h
                    low_ref[pair, rows, im] = im_l
        for store in stores(pair):
            store.start()

    @pl.loop(0, SEGS // 2)
    def _(pair):
        for store in stores(pair):
            store.wait()


def make_replicas(positions, cands, wavenumbers):
    replicas = pltpu.HBM((SEGS // 2, 2 * LANES, 4 * LANES), jnp.bfloat16)
    return pl.pallas_call(
        replica_kernel,
        out_shape=(replicas, replicas),
        in_specs=[in_hbm()] * 3,
        out_specs=(in_hbm(), in_hbm()),
        scratch_shapes=[
            pltpu.VMEM(positions.shape, jnp.float32),
            pltpu.VMEM(cands.shape, jnp.int32),
            pltpu.SMEM(wavenumbers.shape, jnp.float32),
            pltpu.VMEM(replicas.shape, jnp.bfloat16),
            pltpu.VMEM(replicas.shape, jnp.bfloat16),
            pltpu.SemaphoreType.DMA((5,)),
        ],
        compiler_params=pltpu.CompilerParams(vmem_limit_bytes=VMEM_LIMIT),
        cost_estimate=pl.CostEstimate(flops=60_000_000, bytes_accessed=10_000_000, transcendentals=1_000_000),
        name="replicas",
    )(*[keep_in_hbm(array) for array in (positions, cands, wavenumbers)])


def message_kernel(order_ref, spec_ref, high_hbm, low_hbm, out_ref, held, high_ref, low_ref, sem):
    zh = lax.axis_index("zh")

    def loads(some):
        two = pl.ds(some * 2, 2)
        return [
            pltpu.make_async_copy(src.at[two], dst.at[two], sem.at[n, some])
            for n, (src, dst) in enumerate(((high_hbm, high_ref), (low_hbm, low_ref)))
        ]

    for some in range(SEGS // 4):
        for load in loads(some):
            load.start()
    proj = jnp.zeros((ROWS, 4 * LANES), jnp.float32)
    for some in range(SEGS // 4):
        for seg in range(some * 4, some * 4 + 4):
            index = jnp.broadcast_to(order_ref[seg:seg + 1, :], (8, LANES))
            lane = index % LANES
            home = index // LANES
            total = [jnp.zeros((8, LANES), jnp.float32) for _ in range(ROWS // 8)]
            for run in range(SEGS):
                here = home == tile_of(run)
                for part in range(ROWS // 8):
                    there = jnp.take_along_axis(spec_ref[run, part * 8:part * 8 + 8, :], lane, axis=1)
                    total[part] = jnp.where(here, there, total[part])
            for part in range(ROWS // 8):
                held[seg, part * 8:part * 8 + 8, :] = total[part]
        for load in loads(some):
            load.wait()
        for pair in range(some * 2, some * 2 + 2):
            data = jnp.concatenate([spec_ref[pair * 2], spec_ref[pair * 2 + 1]], axis=1)
            data_h, data_l = split(data)
            both = jnp.concatenate([data_h, data_l], axis=0)
            first = jnp.dot(both, high_ref[pair], preferred_element_type=jnp.float32)
            second = jnp.dot(data_h, low_ref[pair], preferred_element_type=jnp.float32)
            proj += first[:ROWS] + first[ROWS:] + second

    powers = []
    for xl in range(2):
        real = proj[:, xl * 2 * LANES:xl * 2 * LANES + LANES]
        value = real + swap_pairs(proj[:, xl * 2 * LANES + LANES:xl * 2 * LANES + 2 * LANES])
        powers.append(jnp.sum(value * value, axis=0, keepdims=True))
    for peer, (y, xl, xh, zl, core) in enumerate(PEER):
        start = peer * MSG
        out_ref[start:start + ROWS, :] = held[xl * 16 + zh * 4 + zl * 2 + core]
        for run in range(2):
            place = slice(start + (1 + run) * ROWS, start + (2 + run) * ROWS)
            out_ref[place, :] = held[(y * 2 + xh) * 4 + core * 2 + run]
        out_ref[start + 3 * ROWS:start + MSG, :] = jnp.broadcast_to(powers[xl], (MSG - 3 * ROWS, LANES))


def make_messages(order, spec, high, low):
    return pl.pallas_call(
        message_kernel,
        out_shape=jax.ShapeDtypeStruct((PEERS * MSG, LANES), jnp.float32),
        in_specs=[in_vmem(), in_vmem(), in_hbm(), in_hbm()],
        out_specs=in_vmem(),
        scratch_shapes=[
            pltpu.VMEM((SEGS, ROWS, LANES), jnp.float32),
            pltpu.VMEM(high.shape, high.dtype),
            pltpu.VMEM(low.shape, low.dtype),
            pltpu.SemaphoreType.DMA((2, SEGS // 4)),
        ],
        compiler_params=pltpu.CompilerParams(vmem_limit_bytes=VMEM_LIMIT),
        cost_estimate=pl.CostEstimate(flops=100_000_000, bytes_accessed=10_000_000, transcendentals=0),
        name="messages",
    )(order, spec, keep_in_hbm(high), keep_in_hbm(low))


def gather_rows(ref, freq, start):
    each = ref.shape[0] // PEERS
    return jnp.concatenate([ref[n * each + start:n * each + start + ROWS, :] for n in HOLDERS[freq]], axis=0)


def product(left_h, left_l, ref, freq, start):
    parts = [gather_rows(ref, freq, start + run * ROWS) for run in range(2)]
    right_h, right_l = split(jnp.concatenate(parts, axis=1))
    total = jnp.dot(left_h, right_h, preferred_element_type=jnp.float32)
    total += jnp.dot(left_h, right_l, preferred_element_type=jnp.float32)
    return total + jnp.dot(left_l, right_h, preferred_element_type=jnp.float32)


def send_out(freq, half, total, stage, out_ref, sem):
    stage[freq, 0] = total[:LANES]
    stage[freq, 1] = total[LANES:]
    columns = pl.ds(pl.multiple_of(half * 2 * LANES, 2 * LANES), 2 * LANES)
    copy = pltpu.make_async_copy(stage.at[freq], out_ref.at[freq, :, :, columns], sem.at[freq])
    copy.start()
    return copy


def own_density_kernel(got_ref, out_ref, high_ref, low_ref, stage, sem):
    copies = []
    for freq in range(4):
        rows = gather_rows(got_ref, freq, 0) * (1.0 / WINDOWS)
        left = jnp.concatenate([rows, swap_pairs(rows)], axis=1)
        left_h, left_l = split(left.T)
        high_ref[freq] = left_h
        low_ref[freq] = left_l
        total = product(left_h, left_l, got_ref, freq, ROWS)
        copies.append(send_out(freq, lax.axis_index("core"), total, stage, out_ref, sem))
    for copy in copies:
        copy.wait()


def other_density_kernel(high_ref, low_ref, got_ref, base_ref, out_ref, stage, sem):
    del base_ref
    copies = []
    for freq in range(4):
        total = product(high_ref[freq], low_ref[freq], got_ref, freq, 0)
        copies.append(send_out(freq, 1 - lax.axis_index("core"), total, stage, out_ref, sem))
    for copy in copies:
        copy.wait()


def make_density(received, columns):
    density = jax.ShapeDtypeStruct((4, 2, LANES, 4 * LANES), jnp.float32)
    left = jax.ShapeDtypeStruct((4, 2 * LANES, 2 * LANES), jnp.bfloat16)
    scratch = [pltpu.VMEM((4, 2, LANES, 2 * LANES), jnp.float32), pltpu.SemaphoreType.DMA((4,))]
    params = pltpu.CompilerParams(vmem_limit_bytes=VMEM_LIMIT)
    cost = pl.CostEstimate(flops=800_000_000, bytes_accessed=5_000_000, transcendentals=0)
    anywhere = in_hbm()
    half, high, low = pl.pallas_call(
        own_density_kernel,
        out_shape=(density, left, left),
        in_specs=[in_vmem()],
        out_specs=(anywhere, in_vmem(), in_vmem()),
        scratch_shapes=scratch,
        compiler_params=params,
        cost_estimate=cost,
        name="own_density",
    )(received)
    other = lax.ppermute(columns, "core", [(0, 1), (1, 0)])
    return pl.pallas_call(
        other_density_kernel,
        out_shape=density,
        in_specs=[in_vmem(), in_vmem(), in_vmem(), anywhere],
        out_specs=anywhere,
        scratch_shapes=scratch,
        input_output_aliases={3: 0},
        compiler_params=params,
        cost_estimate=cost,
        name="other_density",
    )(high, low, other, half)


def norms_of(positions, cands):
    cand_x = ((cands % GRID_SIDE).astype(jnp.float32) - GRID_SIDE / 2) * 8.0
    cand_z = 50.0 + (cands // GRID_SIDE).astype(jnp.float32) * 4.0
    delta = positions[0] - cand_x[..., None]
    r2 = delta * delta + positions[1] * positions[1] + (cand_z * cand_z)[..., None]
    return jnp.sum(1.0 / r2, axis=-1)


def local(spectra, sensor_positions, wavenumbers, sensor_order, candidates):
    parts = spectra.reshape(2, 2, 1, 2, ROWS, LANES)
    outgoing = jnp.broadcast_to(parts, (2, 2, 4, 2, ROWS, LANES))
    gathered = lax.all_to_all(outgoing.reshape(SEGS, ROWS, LANES), GATHER, 0, 0, tiled=True)
    high, low = make_replicas(sensor_positions, candidates, wavenumbers)
    messages = make_messages(sensor_order.reshape(SEGS, LANES), gathered, high, low)
    received = lax.all_to_all(messages.reshape(PEERS, MSG // 2, 2, LANES), SPREAD, 0, 0, tiled=True)
    columns = received[:, ROWS // 2:3 * ROWS // 2].reshape(PEERS * 2 * ROWS, LANES)
    density = make_density(received.reshape(PEERS * MSG, LANES), columns)
    shares = received[:, 3 * ROWS // 2, 0, :].reshape(4, 2, 2, 2, 2, LANES)
    powers = jnp.sum(shares, axis=(0, 2, 3)).swapaxes(0, 1).reshape(4, LANES)
    win = lax.axis_index(WIN)
    power = lax.dynamic_slice_in_dim(powers, (lax.axis_index(("zl", "core")) * 8 + win) * 4, 4, 1)
    candidates, _ = lax.optimization_barrier((candidates, power))
    owned = lax.dynamic_slice_in_dim(candidates, (lax.axis_index(TILE) * 8 + win) * 4, 4, 1)
    beam = power / (WINDOWS * norms_of(sensor_positions, owned))
    return (density, beam)


def solution(mesh):
    fine = Mesh(mesh.devices.reshape(SIZES), NAMES)
    in_specs = (P(None, WIN, None, TILE), P(), P(), P(), P())
    out_specs = (P(None, None, TILE, WIN), P(None, TILE + WIN))
    return jax.shard_map(local, mesh=fine, in_specs=in_specs, out_specs=out_specs, check_vma=False)
```

time: 537 us -> 68.5 us (0.13); the launches traced: 529 us -> 68.1 us
  matrix products: 150 us -> 0 us
  local copies, waits for them, and re-layouts: 106 us -> 2.72 us
  blocking collectives: 115 us -> 34.3 us
  other arithmetic: 80.4 us -> 1.76 us
  waiting for transfers between devices: 56.4 us -> 1.37 us
  Pallas kernels: 0 us -> 16.2 us
  between operations: 14.5 us -> 0.72 us
    dot_general x8 -> x0, matrix products: 150 us -> none  [the longest x1 48.8 us: local(): jnp.einsum('fij,fjc->fic', dens_re, col_im, precision=hp)]
    unnamed x1 -> x0, blocking collectives: 80.4 us -> none
    all_gather x1 -> x0, waiting for transfers between devices: 56.3 us -> none  [local(): gathered = lax.all_gather(spectra, 'tile', axis=3, tiled=True)]
    gather x5 -> x0, local copies, waits for them, and re-layouts: 52.9 us -> none  [the longest x1 44.4 us: local(): ordered = jnp.take(gathered, sensor_order, axis=3)]
    unnamed x14 -> x4, local copies, waits for them, and re-layouts: 37.9 us -> 0.01 us
    all_gather x1 -> x0, blocking collectives: 34.9 us -> none  [local(): all_rows = lax.all_gather(row_block, 'win', axis=1, tiled=True)]
    all_to_all x0 -> x1, blocking collectives: none -> 34.3 us  [local(): lax.all_to_all(messages.reshape(PEERS, MSG // 2, 2, LANES), SPREAD, 0, 0,...]
    dot_general x1 -> x0, other arithmetic: 33.2 us -> none  [local(): jnp.einsum('fij,fjc->fic', dens_im, col_im, precision=hp)]
  transfers between devices with their start and end apart: 2 -> 2, of which waited for: 1 -> 1; matrix products, arithmetic and copies ran while one was open for 12% -> 3% of each run, Pallas kernels for 0% -> 15%
where the time goes in v2:
time: 68.5 us; the launch traced here: 68.1 us
  blocking collectives  34.3 us (50%)
  Pallas kernels  16.2 us (24%)
  starting transfers between devices  11.1 us (16%)
  local copies, waits for them, and re-layouts  2.72 us (4%)
  other arithmetic  1.76 us (3%)
  waiting for transfers between devices  1.37 us (2%)
  between operations  0.72 us (1%)
    all_to_all x1, blocking collectives, local(): lax.all_to_all(messages.reshape(PEERS, MSG // 2, 2, LANES), SPREAD, 0, 0,...  34.3 us
    all_to_all x1, starting transfers between devices, local(): lax.all_to_all(outgoing.reshape(SEGS, ROWS, LANES), GATHER, 0, 0, tiled=T...  11.1 us
    pallas_call x1, Pallas kernels, make_replicas(): pl.pallas_call(replica_kernel, out_shape=(replicas, replicas), in_specs=[...  8.91 us
    pallas_call x1, Pallas kernels, make_messages(): pl.pallas_call(message_kernel, out_shape=jax.ShapeDtypeStruct((PEERS * MS...  4.35 us
    broadcast_in_dim x1, local copies, waits for them, and re-layouts, local(): outgoing = jnp.broadcast_to(parts, (2, 2, 4, 2, ROWS, LANES))  1.57 us
    pallas_call x1, Pallas kernels, make_density(): pl.pallas_call(own_density_kernel, out_shape=(density, left, left), in_sp...  1.53 us
    pallas_call x1, Pallas kernels, make_density(): pl.pallas_call(other_density_kernel, out_shape=density, in_specs=[in_vmem...  1.42 us
  transfers between devices with their start and end apart: 2, of which 1 were waited for; matrix products, arithmetic and copies ran while one was open for 3% of the time, Pallas kernels for 15%

profile of v2, /device:TPU:1, one launch (start us, length us, event | category | flops | bytes accessed | tf_op | source)
XLA Modules:
  0.0 68.1 jit_solution(11665439093371242761)
XLA Ops:
  0.6 0.0 copy-start
  0.6 1.6 %broadcast_in_dim.5 = f32[2,2,4,2,16,128]{5,4,3,2,1,0:T(8,128)} broadcast(f32[2,2,2,16,128]{4,3,2,1,0:T(8,128)} %bitcast.15), dimensions={0,1,3,4,5} | broadcast | bytes 327680 | tf_op jit(solution)/shard_map/broadcast_in_dim | solution.py:319
  2.2 11.1 %all-to-all-start = ((f32[32,16,128]{2,1,0:T(8,128)}), f32[32,16,128]{2,1,0:T(8,128)S(1)}, u32[]{:S(2)}, u32[]{:S(2)}) async-start(f32[32,16,128]{2,1,0:T(8,128)} %bitcast.2), calls=%async_computation | async-start | bytes 524288 | tf_op jit(solution)/shard_map/all_to_all | solution.py:320
  13.3 8.9 %replicas.1 = (bf16[16,256,512]{2,1,0:T(8,128)(2,1)}, bf16[16,256,512]{2,1,0:T(8,128)(2,1)}) custom-call(f32[2,4096]{1,0:T(2,128)} %pos_hbm.1, s32[4,1024]{1,0:T(4,128)} %cand_hbm.1, f32[4]{0:T(128)} %wave_hbm.1), custom_call_target="tpu_custom_call" | custom-call | flops 60000000 | bytes 10000000 | tf_op jit(solution)/shard_map/replicas/pallas_call | solution.py:144
  22.2 1.4 %all-to-all-done.spec_ref = f32[32,16,128]{2,1,0:T(8,128)S(1)} async-done(((f32[32,16,128]{2,1,0:T(8,128)}), f32[32,16,128]{2,1,0:T(8,128)S(1)}, u32[]{:S(2)}, u32[]{:S(2)}) %all-to-all-start) | async-done | bytes 262176 | tf_op jit(solution)/shard_map/all_to_all | solution.py:320
  23.6 0.0 copy-done
  23.6 4.3 %messages.1 = f32[3200,128]{1,0:T(8,128)S(1)} custom-call(s32[32,128]{1,0:T(8,128)S(1)} %bitcast.13, f32[32,16,128]{2,1,0:T(8,128)S(1)} %all-to-all-done.spec_ref, bf16[16,256,512]{2,1,0:T(8,128)(2,1)} %get-tuple-element.8.high_hbm, bf16[16,256,512]{2,1,0:T(8,128)(2,1)} %get-tuple-element.9.low_hbm), custom_call_target="tpu_custom_call" | custom-call | flops 100000000 | bytes 10000000 | tf_op jit(solution)/shard_map/messages/pallas_call | solution.py:215
  27.9 0.0 copy-start.1
  27.9 34.3 %all_to_all.10 = f32[64,25,2,128]{3,2,1,0:T(2,128)S(1)} all-to-all(f32[64,25,2,128]{3,2,1,0:T(2,128)S(1)} %bitcast.11), channel_id=1, replica_groups=mesh['xl'=2,'zh'=4,'zl'=2,'core'=2,'y'=4,'xh'=2] {'y','xl','xh','zl','co..., dimensions={0} | all-to-all | bytes 3276800 | tf_op jit(solution)/shard_map/all_to_all | solution.py:323
  62.2 1.1 %slice.17 = f32[64,16,2,128]{3,2,1,0:T(2,128)} slice(f32[64,25,2,128]{3,2,1,0:T(2,128)S(1)} %all_to_all.10), slice={[0:64], [8:24], [0:2], [0:128]} | slice | bytes 2097152 | tf_op jit(solution)/shard_map/slice | solution.py:324
  63.3 0.0 collective-permute-start
  63.3 0.0 copy-done.1
  63.4 1.5 %own_density.1 = (f32[4,2,128,512]{3,2,1,0:T(8,128)}, bf16[4,256,256]{2,1,0:T(8,128)(2,1)S(1)}, bf16[4,256,256]{2,1,0:T(8,128)(2,1)S(1)}) custom-call(f32[3200,128]{1,0:T(8,128)S(1)} %bitcast.12), custom_call_target="tpu_custom_call" | custom-call | flops 800000000 | bytes 5000000 | tf_op jit(solution)/shard_map/own_density/pallas_call | solution.py:285
  65.0 0.8 %fusion.3 = (f32[4,4]{1,0:T(4,128)S(1)}, f32[4,4]{1,0:T(4,128)S(1)}) fusion(s32[4,1024]{1,0:T(4,128)} %cand_hbm.1, s32[]{:T(128)S(6)} %select_n.19), kind=kLoop, calls=%fused_computation.10 | loop fusion | flops 416 | bytes 196 | tf_op jit(solution)/shard_map/mul | solution.py:310
  65.8 0.3 fusion
  66.0 0.7 multiply_divide_fusion
  66.7 0.0 collective-permute-done.got_ref
  66.7 1.4 %other_density.1 = f32[4,2,128,512]{3,2,1,0:T(8,128)} custom-call(bf16[4,256,256]{2,1,0:T(8,128)(2,1)S(1)} %get-tuple-element.10.high_ref, bf16[4,256,256]{2,1,0:T(8,128)(2,1)S(1)} %get-tuple-element.11.low_ref, f32[2048,128]{1,0:T(8,128)S(1)} %collective-permute-done.got_ref, ...), custom_call_target="tpu_custom_call", output_to_operand_aliasing={{}: (3, {})} | custom-call | flops 800000000 | bytes 5000000 | tf_op jit(solution)/shard_map/other_density/pallas_call | solution.py:296
  (4 shorter events, 0.1 us)
Async XLA Ops:
  0.6 22.9 %copy-start = (s32[4096]{0:T(1024)S(1)}, s32[4096]{0:T(1024)}, u32[]{:S(2)}) copy-start(s32[4096]{0:T(1024)} %param.8) | copy-start | bytes 49156
  2.2 21.4 %all-to-all-start = ((f32[32,16,128]{2,1,0:T(8,128)}), f32[32,16,128]{2,1,0:T(8,128)S(1)}, u32[]{:S(2)}, u32[]{:S(2)}) async-start(f32[32,16,128]{2,1,0:T(8,128)} %bitcast.2), calls=%async_computation | async-start | bytes 524288 | tf_op jit(solution)/shard_map/all_to_all | solution.py:320
  27.9 35.4 %copy-start.1 = (f32[2,4096]{1,0:T(2,128)S(1)}, f32[2,4096]{1,0:T(2,128)}, u32[]{:S(2)}) copy-start(f32[2,4096]{1,0:T(2,128)} %pos_hbm.1) | copy-start | bytes 98308
  63.3 3.4 %collective-permute-start = (f32[2048,128]{1,0:T(8,128)}, f32[2048,128]{1,0:T(8,128)S(1)}, u32[]{:S(2)}, u32[]{:S(2)}) collective-permute-start(f32[2048,128]{1,0:T(8,128)} %bitcast.5), channel_id=1, source_target_pairs={{0,8},{8,0},{1,9},{9,1},{2,10},{10,2},{3,11},{11,3},{4,12},{12,4},... | collective-permute-start | bytes 3145736 | tf_op jit(solution)/shard_map/ppermute | solution.py:295

commit v3 on v2

--- a/solution.py
+++ b/solution.py
@@ -14,6 +14,9 @@
 PEERS = 64
 MSG = 3 * ROWS + 2
 VMEM_LIMIT = 24 * 1024 * 1024
+UNROLL = 4
+PAIRS = SEGS // 2
+HELD = 6
 NAMES = ("xl", "zh", "zl", "core", "y", "xh")
 SIZES = (2, 4, 2, 2, 4, 2)
 TILE = ("xl", "zh", "zl", "core")
@@ -78,9 +81,9 @@
     return jnp.where(row % 2 == 0, up, -down)
 
 
-def replica_kernel(pos_hbm, cand_hbm, wave_hbm, high_hbm, low_hbm, pos_ref, cand_ref, wave_ref, high_ref, low_ref, sem):
+def replica_kernel(pos_hbm, cand_hbm, wave_hbm, held_ref, rest_hbm, scale_ref, pos_ref, cand_ref, wave_ref, rest_ref, sem):
     pairs = ((pos_hbm, pos_ref), (cand_hbm, cand_ref), (wave_hbm, wave_ref))
-    loads = [pltpu.make_async_copy(src, dst, sem.at[2 + n]) for n, (src, dst) in enumerate(pairs)]
+    loads = [pltpu.make_async_copy(src, dst, sem.at[n]) for n, (src, dst) in enumerate(pairs)]
     for load in loads:
         load.start()
     for load in loads:
@@ -97,14 +100,11 @@
         depth = 50.0 + (grid // GRID_SIDE).astype(jnp.float32) * 4.0
         cz2.append(depth * depth)
 
-    def stores(pair):
-        return [
-            pltpu.make_async_copy(src.at[pair], dst.at[pair], sem.at[n])
-            for n, (src, dst) in enumerate(((high_ref, high_hbm), (low_ref, low_hbm)))
-        ]
-
-    @pl.loop(0, SEGS // 2)
-    def _(pair):
+    def store(pair):
+        return pltpu.make_async_copy(rest_ref.at[pair], rest_hbm.at[pair], sem.at[3])
+
+    def pair_step(pair, out_ref, out_pair, norms):
+        norms = list(norms)
         for half in range(2):
             lanes = pl.ds(pl.multiple_of(tile_of(pair * 2 + half) * LANES, LANES), LANES)
             px = jnp.broadcast_to(pos_ref[0:1, lanes], (LANES, LANES)).T
@@ -126,33 +126,45 @@
                     rows = slice(half * LANES + part * 32, half * LANES + part * 32 + 32)
                     re = slice(xl * 2 * LANES, xl * 2 * LANES + LANES)
                     im = slice(xl * 2 * LANES + LANES, xl * 2 * LANES + 2 * LANES)
-                    high_ref[pair, rows, re] = re_h
-                    low_ref[pair, rows, re] = re_l
-                    high_ref[pair, rows, im] = im_h
-                    low_ref[pair, rows, im] = im_l
-        for store in stores(pair):
-            store.start()
-
-    @pl.loop(0, SEGS // 2)
+                    out_ref[out_pair, 0, rows, re] = re_h
+                    out_ref[out_pair, 1, rows, re] = re_l
+                    out_ref[out_pair, 0, rows, im] = im_h
+                    out_ref[out_pair, 1, rows, im] = im_l
+                    amp2 = inv * inv
+                    norms[xl] += (amp2[0:8] + amp2[8:16]) + (amp2[16:24] + amp2[24:32])
+        return tuple(norms)
+
+    def rest_step(pair, norms):
+        norms = pair_step(pair + HELD, rest_ref, pair, norms)
+        store(pair).start()
+        return norms
+
+    norms = (jnp.zeros((8, LANES), jnp.float32),) * 2
+    norms = lax.fori_loop(0, PAIRS - HELD, rest_step, norms, unroll=UNROLL)
+    norms = lax.fori_loop(0, HELD, lambda pair, norms: pair_step(pair, held_ref, pair, norms), norms, unroll=UNROLL)
+    for xl in range(2):
+        norm = jnp.sum(norms[xl], axis=0, keepdims=True)
+        scale_ref[xl] = jnp.broadcast_to(1.0 / (WINDOWS * norm), (8, LANES))
+
+    @pl.loop(0, PAIRS - HELD)
     def _(pair):
-        for store in stores(pair):
-            store.wait()
+        store(pair).wait()
 
 
 def make_replicas(positions, cands, wavenumbers):
-    replicas = pltpu.HBM((SEGS // 2, 2 * LANES, 4 * LANES), jnp.bfloat16)
+    held = jax.ShapeDtypeStruct((HELD, 2, 2 * LANES, 4 * LANES), jnp.bfloat16)
+    rest = pltpu.HBM((PAIRS - HELD, 2, 2 * LANES, 4 * LANES), jnp.bfloat16)
     return pl.pallas_call(
         replica_kernel,
-        out_shape=(replicas, replicas),
+        out_shape=(held, rest, jax.ShapeDtypeStruct((2, 8, LANES), jnp.float32)),
         in_specs=[in_hbm()] * 3,
-        out_specs=(in_hbm(), in_hbm()),
+        out_specs=(in_vmem(), in_hbm(), in_vmem()),
         scratch_shapes=[
             pltpu.VMEM(positions.shape, jnp.float32),
             pltpu.VMEM(cands.shape, jnp.int32),
             pltpu.SMEM(wavenumbers.shape, jnp.float32),
-            pltpu.VMEM(replicas.shape, jnp.bfloat16),
-            pltpu.VMEM(replicas.shape, jnp.bfloat16),
-            pltpu.SemaphoreType.DMA((5,)),
+            pltpu.VMEM(rest.shape, jnp.bfloat16),
+            pltpu.SemaphoreType.DMA((4,)),
         ],
         compiler_params=pltpu.CompilerParams(vmem_limit_bytes=VMEM_LIMIT),
         cost_estimate=pl.CostEstimate(flops=60_000_000, bytes_accessed=10_000_000, transcendentals=1_000_000),
@@ -160,19 +172,11 @@
     )(*[keep_in_hbm(array) for array in (positions, cands, wavenumbers)])
 
 
-def message_kernel(order_ref, spec_ref, high_hbm, low_hbm, out_ref, held, high_ref, low_ref, sem):
+def message_kernel(order_ref, spec_ref, held_ref, rest_hbm, scale_ref, out_ref, ordered, rest_ref, sem):
     zh = lax.axis_index("zh")
-
-    def loads(some):
-        two = pl.ds(some * 2, 2)
-        return [
-            pltpu.make_async_copy(src.at[two], dst.at[two], sem.at[n, some])
-            for n, (src, dst) in enumerate(((high_hbm, high_ref), (low_hbm, low_ref)))
-        ]
-
-    for some in range(SEGS // 4):
-        for load in loads(some):
-            load.start()
+    loads = [pltpu.make_async_copy(rest_hbm.at[n], rest_ref.at[n], sem.at[n]) for n in range(PAIRS - HELD)]
+    for load in loads:
+        load.start()
     proj = jnp.zeros((ROWS, 4 * LANES), jnp.float32)
     for some in range(SEGS // 4):
         for seg in range(some * 4, some * 4 + 4):
@@ -186,47 +190,49 @@
                     there = jnp.take_along_axis(spec_ref[run, part * 8:part * 8 + 8, :], lane, axis=1)
                     total[part] = jnp.where(here, there, total[part])
             for part in range(ROWS // 8):
-                held[seg, part * 8:part * 8 + 8, :] = total[part]
-        for load in loads(some):
-            load.wait()
+                ordered[seg, part * 8:part * 8 + 8, :] = total[part]
         for pair in range(some * 2, some * 2 + 2):
             data = jnp.concatenate([spec_ref[pair * 2], spec_ref[pair * 2 + 1]], axis=1)
             data_h, data_l = split(data)
             both = jnp.concatenate([data_h, data_l], axis=0)
-            first = jnp.dot(both, high_ref[pair], preferred_element_type=jnp.float32)
-            second = jnp.dot(data_h, low_ref[pair], preferred_element_type=jnp.float32)
+            if pair < HELD:
+                high, low = held_ref[pair, 0], held_ref[pair, 1]
+            else:
+                loads[pair - HELD].wait()
+                high, low = rest_ref[pair - HELD, 0], rest_ref[pair - HELD, 1]
+            first = jnp.dot(both, high, preferred_element_type=jnp.float32)
+            second = jnp.dot(data_h, low, preferred_element_type=jnp.float32)
             proj += first[:ROWS] + first[ROWS:] + second
 
     powers = []
     for xl in range(2):
         real = proj[:, xl * 2 * LANES:xl * 2 * LANES + LANES]
         value = real + swap_pairs(proj[:, xl * 2 * LANES + LANES:xl * 2 * LANES + 2 * LANES])
-        powers.append(jnp.sum(value * value, axis=0, keepdims=True))
+        powers.append(jnp.sum(value * value, axis=0, keepdims=True) * scale_ref[xl, 0:1, :])
     for peer, (y, xl, xh, zl, core) in enumerate(PEER):
         start = peer * MSG
-        out_ref[start:start + ROWS, :] = held[xl * 16 + zh * 4 + zl * 2 + core]
+        out_ref[start:start + ROWS, :] = ordered[xl * 16 + zh * 4 + zl * 2 + core]
         for run in range(2):
             place = slice(start + (1 + run) * ROWS, start + (2 + run) * ROWS)
-            out_ref[place, :] = held[(y * 2 + xh) * 4 + core * 2 + run]
+            out_ref[place, :] = ordered[(y * 2 + xh) * 4 + core * 2 + run]
         out_ref[start + 3 * ROWS:start + MSG, :] = jnp.broadcast_to(powers[xl], (MSG - 3 * ROWS, LANES))
 
 
-def make_messages(order, spec, high, low):
+def make_messages(order, spec, held, rest, scale):
     return pl.pallas_call(
         message_kernel,
         out_shape=jax.ShapeDtypeStruct((PEERS * MSG, LANES), jnp.float32),
-        in_specs=[in_vmem(), in_vmem(), in_hbm(), in_hbm()],
+        in_specs=[in_vmem(), in_vmem(), in_vmem(), in_hbm(), in_vmem()],
         out_specs=in_vmem(),
         scratch_shapes=[
             pltpu.VMEM((SEGS, ROWS, LANES), jnp.float32),
-            pltpu.VMEM(high.shape, high.dtype),
-            pltpu.VMEM(low.shape, low.dtype),
-            pltpu.SemaphoreType.DMA((2, SEGS // 4)),
+            pltpu.VMEM(rest.shape, rest.dtype),
+            pltpu.SemaphoreType.DMA((PAIRS - HELD,)),
         ],
         compiler_params=pltpu.CompilerParams(vmem_limit_bytes=VMEM_LIMIT),
         cost_estimate=pl.CostEstimate(flops=100_000_000, bytes_accessed=10_000_000, transcendentals=0),
         name="messages",
-    )(order, spec, keep_in_hbm(high), keep_in_hbm(low))
+    )(order, spec, held, keep_in_hbm(rest), scale)
 
 
 def gather_rows(ref, freq, start):
@@ -251,7 +257,29 @@
     return copy
 
 
-def own_density_kernel(got_ref, out_ref, high_ref, low_ref, stage, sem):
+def column_kernel(got_ref, out_ref):
+    for n in range(PEERS):
+        out_ref[n * 2 * ROWS:(n + 1) * 2 * ROWS, :] = got_ref[n * MSG + ROWS:n * MSG + 3 * ROWS, :]
+
+
+def take_columns(received):
+    return pl.pallas_call(
+        column_kernel,
+        out_shape=jax.ShapeDtypeStruct((PEERS * 2 * ROWS, LANES), jnp.float32),
+        in_specs=[in_vmem()],
+        out_specs=in_vmem(),
+        compiler_params=pltpu.CompilerParams(vmem_limit_bytes=VMEM_LIMIT),
+        name="columns",
+    )(received)
+
+
+def own_density_kernel(got_ref, out_ref, high_ref, low_ref, beam_ref, stage, sem):
+    mine = (lax.axis_index(("zl", "core")) * 8 + lax.axis_index(WIN)) * 4
+    for freq in range(4):
+        shares = [got_ref[n * MSG + 3 * ROWS:n * MSG + 3 * ROWS + 1, :] for n in HOLDERS[freq]]
+        while len(shares) > 1:
+            shares = [a + b for a, b in zip(shares[::2], shares[1::2])]
+        beam_ref[freq:freq + 1, :] = pltpu.roll(shares[0], lax.rem(LANES - mine, LANES), 1)[:, 0:4]
     copies = []
     for freq in range(4):
         rows = gather_rows(got_ref, freq, 0) * (1.0 / WINDOWS)
@@ -275,25 +303,25 @@
         copy.wait()
 
 
-def make_density(received, columns):
+def make_density(received):
     density = jax.ShapeDtypeStruct((4, 2, LANES, 4 * LANES), jnp.float32)
     left = jax.ShapeDtypeStruct((4, 2 * LANES, 2 * LANES), jnp.bfloat16)
     scratch = [pltpu.VMEM((4, 2, LANES, 2 * LANES), jnp.float32), pltpu.SemaphoreType.DMA((4,))]
     params = pltpu.CompilerParams(vmem_limit_bytes=VMEM_LIMIT)
     cost = pl.CostEstimate(flops=800_000_000, bytes_accessed=5_000_000, transcendentals=0)
     anywhere = in_hbm()
-    half, high, low = pl.pallas_call(
+    half, high, low, beam = pl.pallas_call(
         own_density_kernel,
-        out_shape=(density, left, left),
+        out_shape=(density, left, left, jax.ShapeDtypeStruct((4, 4), jnp.float32)),
         in_specs=[in_vmem()],
-        out_specs=(anywhere, in_vmem(), in_vmem()),
+        out_specs=(anywhere, in_vmem(), in_vmem(), in_vmem()),
         scratch_shapes=scratch,
         compiler_params=params,
         cost_estimate=cost,
         name="own_density",
     )(received)
-    other = lax.ppermute(columns, "core", [(0, 1), (1, 0)])
-    return pl.pallas_call(
+    other = lax.ppermute(take_columns(received), "core", [(0, 1), (1, 0)])
+    density = pl.pallas_call(
         other_density_kernel,
         out_shape=density,
         in_specs=[in_vmem(), in_vmem(), in_vmem(), anywhere],
@@ -304,33 +332,17 @@
         cost_estimate=cost,
         name="other_density",
     )(high, low, other, half)
-
-
-def norms_of(positions, cands):
-    cand_x = ((cands % GRID_SIDE).astype(jnp.float32) - GRID_SIDE / 2) * 8.0
-    cand_z = 50.0 + (cands // GRID_SIDE).astype(jnp.float32) * 4.0
-    delta = positions[0] - cand_x[..., None]
-    r2 = delta * delta + positions[1] * positions[1] + (cand_z * cand_z)[..., None]
-    return jnp.sum(1.0 / r2, axis=-1)
+    return density, beam
 
 
 def local(spectra, sensor_positions, wavenumbers, sensor_order, candidates):
     parts = spectra.reshape(2, 2, 1, 2, ROWS, LANES)
     outgoing = jnp.broadcast_to(parts, (2, 2, 4, 2, ROWS, LANES))
     gathered = lax.all_to_all(outgoing.reshape(SEGS, ROWS, LANES), GATHER, 0, 0, tiled=True)
-    high, low = make_replicas(sensor_positions, candidates, wavenumbers)
-    messages = make_messages(sensor_order.reshape(SEGS, LANES), gathered, high, low)
+    held, rest, scale = make_replicas(sensor_positions, candidates, wavenumbers)
+    messages = make_messages(sensor_order.reshape(SEGS, LANES), gathered, held, rest, scale)
     received = lax.all_to_all(messages.reshape(PEERS, MSG // 2, 2, LANES), SPREAD, 0, 0, tiled=True)
-    columns = received[:, ROWS // 2:3 * ROWS // 2].reshape(PEERS * 2 * ROWS, LANES)
-    density = make_density(received.reshape(PEERS * MSG, LANES), columns)
-    shares = received[:, 3 * ROWS // 2, 0, :].reshape(4, 2, 2, 2, 2, LANES)
-    powers = jnp.sum(shares, axis=(0, 2, 3)).swapaxes(0, 1).reshape(4, LANES)
-    win = lax.axis_index(WIN)
-    power = lax.dynamic_slice_in_dim(powers, (lax.axis_index(("zl", "core")) * 8 + win) * 4, 4, 1)
-    candidates, _ = lax.optimization_barrier((candidates, power))
-    owned = lax.dynamic_slice_in_dim(candidates, (lax.axis_index(TILE) * 8 + win) * 4, 4, 1)
-    beam = power / (WINDOWS * norms_of(sensor_positions, owned))
-    return (density, beam)
+    return make_density(received.reshape(PEERS * MSG, LANES))
 
 
 def solution(mesh):

time: 68.5 us -> 65.9 us (0.962)
  waiting for transfers between devices: 1.37 us -> 3.35 us
  other arithmetic: 1.76 us -> 0 us
  Pallas kernels: 16.2 us -> 14.5 us
  local copies, waits for them, and re-layouts: 2.72 us -> 1.58 us
    all_to_all x1, waiting for transfers between devices: 1.37 us -> 2.82 us  [local(): lax.all_to_all(outgoing.reshape(SEGS, ROWS, LANES), GATHER, 0, 0, tiled=T...]
    slice x2 -> x0, local copies, waits for them, and re-layouts: 1.14 us -> none  [the longest x1 1.11 us: local(): received[:, ROWS // 2:3 * ROWS // 2].reshape(PEERS * 2 * ROWS, LANES)]
    pallas_call x1, Pallas kernels: 4.35 us -> 3.48 us  [make_messages(): pl.pallas_call(message_kernel, out_shape=jax.ShapeDtypeStruct((PEERS * MS...]
    pallas_call x2 -> x3, Pallas kernels: 10.4 us -> 9.64 us  [the longest x1 7.46 us: make_replicas(): pl.pallas_call(replica_kernel, out_shape=(held, rest, jax.ShapeDtypeStruc...]
    mul x1 -> x0, other arithmetic: 0.77 us -> none  [norms_of(): cand_x = ((cands % GRID_SIDE).astype(jnp.float32) - GRID_SIDE / 2) * 8.0]
  transfers between devices with their start and end apart: 2 -> 2, of which waited for: 1 -> 2; matrix products, arithmetic and copies ran while one was open for 3% -> 0% of each run, Pallas kernels for 15% -> 15%
where the time goes in v3:
time: 65.9 us; the launch traced here: 65.6 us
  blocking collectives  34.3 us (52%)
  Pallas kernels  14.5 us (22%)
  starting transfers between devices  11.2 us (17%)
  waiting for transfers between devices  3.35 us (5%)
  local copies, waits for them, and re-layouts  1.58 us (2%)
  between operations  0.68 us (1%)
    all_to_all x1, blocking collectives, local(): lax.all_to_all(messages.reshape(PEERS, MSG // 2, 2, LANES), SPREAD, 0, 0,...  34.3 us
    all_to_all x1, starting transfers between devices, local(): lax.all_to_all(outgoing.reshape(SEGS, ROWS, LANES), GATHER, 0, 0, tiled=T...  11.1 us
    pallas_call x1, Pallas kernels, make_replicas(): pl.pallas_call(replica_kernel, out_shape=(held, rest, jax.ShapeDtypeStruc...  7.46 us
    pallas_call x1, Pallas kernels, make_messages(): pl.pallas_call(message_kernel, out_shape=jax.ShapeDtypeStruct((PEERS * MS...  3.48 us
    all_to_all x1, waiting for transfers between devices, local(): lax.all_to_all(outgoing.reshape(SEGS, ROWS, LANES), GATHER, 0, 0, tiled=T...  2.82 us
    pallas_call x1, Pallas kernels, make_density(): pl.pallas_call(own_density_kernel, out_shape=(density, left, left, jax.Sh...  2.11 us
    broadcast_in_dim x1, local copies, waits for them, and re-layouts, local(): outgoing = jnp.broadcast_to(parts, (2, 2, 4, 2, ROWS, LANES))  1.57 us
    pallas_call x1, Pallas kernels, make_density(): pl.pallas_call(other_density_kernel, out_shape=density, in_specs=[in_vmem...  1.42 us
  transfers between devices with their start and end apart: 2, of which 2 were waited for; matrix products, arithmetic and copies ran while one was open for 0% of the time, Pallas kernels for 15%

profile of v3, /device:TPU:1, one launch (start us, length us, event | category | flops | bytes accessed | tf_op | source)
XLA Modules:
  0.0 65.6 jit_solution(3461299731966221927)
XLA Ops:
  0.6 0.0 copy-start
  0.6 1.6 %broadcast_in_dim.8 = f32[2,2,4,2,16,128]{5,4,3,2,1,0:T(8,128)} broadcast(f32[2,2,2,16,128]{4,3,2,1,0:T(8,128)} %bitcast.9), dimensions={0,1,3,4,5} | broadcast | bytes 327680 | tf_op jit(solution)/shard_map/broadcast_in_dim | solution.py:340
  2.2 11.1 %all-to-all-start = ((f32[32,16,128]{2,1,0:T(8,128)}), f32[32,16,128]{2,1,0:T(8,128)S(1)}, u32[]{:S(2)}, u32[]{:S(2)}) async-start(f32[32,16,128]{2,1,0:T(8,128)} %bitcast.2), calls=%async_computation | async-start | bytes 524288 | tf_op jit(solution)/shard_map/all_to_all | solution.py:341
  13.3 7.5 %replicas.1 = (bf16[6,2,256,512]{3,2,1,0:T(8,128)(2,1)S(1)}, bf16[10,2,256,512]{3,2,1,0:T(8,128)(2,1)}, f32[2,8,128]{2,1,0:T(8,128)S(1)}) custom-call(f32[2,4096]{1,0:T(2,128)} %pos_hbm.1, s32[4,1024]{1,0:T(4,128)} %cand_hbm.1, f32[4]{0:T(128)} %wave_hbm.1), custom_call_target="tpu_custom_call" | custom-call | flops 60000000 | bytes 10000000 | tf_op jit(solution)/shard_map/replicas/pallas_call | solution.py:157
  20.8 2.8 %all-to-all-done.spec_ref = f32[32,16,128]{2,1,0:T(8,128)S(1)} async-done(((f32[32,16,128]{2,1,0:T(8,128)}), f32[32,16,128]{2,1,0:T(8,128)S(1)}, u32[]{:S(2)}, u32[]{:S(2)}) %all-to-all-start) | async-done | bytes 262176 | tf_op jit(solution)/shard_map/all_to_all | solution.py:341
  23.6 0.0 copy-done
  23.6 3.5 %messages.1 = f32[3200,128]{1,0:T(8,128)S(1)} custom-call(s32[32,128]{1,0:T(8,128)S(1)} %bitcast.8, f32[32,16,128]{2,1,0:T(8,128)S(1)} %all-to-all-done.spec_ref, bf16[6,2,256,512]{3,2,1,0:T(8,128)(2,1)S(1)} %get-tuple-element.9.held_ref, bf16[10,2,256,512]{3,2,1,0:T(8,128)(2,1)} %get-tuple-element.10.rest_hbm, f32[2,8,128]{2,1,0:T(8,128)S(1)} %get-tuple-element.11.scale_ref), custom_call_target="tpu_custom_call" | custom-call | flops 100000000 | bytes 10000000 | tf_op jit(solution)/shard_map/messages/pallas_call | solution.py:222
  27.1 34.3 %all_to_all.10 = f32[64,25,2,128]{3,2,1,0:T(2,128)S(1)} all-to-all(f32[64,25,2,128]{3,2,1,0:T(2,128)S(1)} %bitcast.7), channel_id=1, replica_groups=mesh['xl'=2,'zh'=4,'zl'=2,'core'=2,'y'=4,'xh'=2] {'y','xl','xh','zl','co..., dimensions={0} | all-to-all | bytes 3276800 | tf_op jit(solution)/shard_map/all_to_all | solution.py:344
  61.3 0.1 columns.1
  61.4 0.1 collective-permute-start
  61.5 2.1 %own_density.1 = (f32[4,2,128,512]{3,2,1,0:T(8,128)}, bf16[4,256,256]{2,1,0:T(8,128)(2,1)S(1)}, bf16[4,256,256]{2,1,0:T(8,128)(2,1)S(1)}, f32[4,4]{1,0:T(4,128)}) custom-call(f32[3200,128]{1,0:T(8,128)S(1)} %bitcast.6), custom_call_target="tpu_custom_call" | custom-call | flops 800000000 | bytes 5000000 | tf_op jit(solution)/shard_map/own_density/pallas_call | solution.py:313
  63.6 0.5 collective-permute-done.got_ref
  64.1 1.4 %other_density.1 = f32[4,2,128,512]{3,2,1,0:T(8,128)} custom-call(bf16[4,256,256]{2,1,0:T(8,128)(2,1)S(1)} %get-tuple-element.12.high_ref, bf16[4,256,256]{2,1,0:T(8,128)(2,1)S(1)} %get-tuple-element.13.low_ref, f32[2048,128]{1,0:T(8,128)S(1)} %collective-permute-done.got_ref, ...), custom_call_target="tpu_custom_call", output_to_operand_aliasing={{}: (3, {})} | custom-call | flops 800000000 | bytes 5000000 | tf_op jit(solution)/shard_map/other_density/pallas_call | solution.py:324
Async XLA Ops:
  0.6 22.9 %copy-start = (s32[4096]{0:T(1024)S(1)}, s32[4096]{0:T(1024)}, u32[]{:S(2)}) copy-start(s32[4096]{0:T(1024)} %param.8) | copy-start | bytes 49156
  2.2 21.4 %all-to-all-start = ((f32[32,16,128]{2,1,0:T(8,128)}), f32[32,16,128]{2,1,0:T(8,128)S(1)}, u32[]{:S(2)}, u32[]{:S(2)}) async-start(f32[32,16,128]{2,1,0:T(8,128)} %bitcast.2), calls=%async_computation | async-start | bytes 524288 | tf_op jit(solution)/shard_map/all_to_all | solution.py:341
  61.4 2.7 %collective-permute-start = (f32[2048,128]{1,0:T(8,128)S(1)}, f32[2048,128]{1,0:T(8,128)S(1)}, u32[]{:S(2)}, u32[]{:S(2)}) collective-permute-start(f32[2048,128]{1,0:T(8,128)S(1)} %columns.1), channel_id=1, source_target_pairs={{0,8},{8,0},{1,9},{9,1},{2,10},{10,2},{3,11},{11,3},{4,12},{12,4},... | collective-permute-start | bytes 3145736 | tf_op jit(solution)/shard_map/ppermute | solution.py:323

commit v4 on v3

--- a/solution.py
+++ b/solution.py
@@ -12,7 +12,7 @@
 SEGS = 32
 ROWS = 16
 PEERS = 64
-MSG = 3 * ROWS + 2
+MSG = 3 * ROWS + 1
 VMEM_LIMIT = 24 * 1024 * 1024
 UNROLL = 4
 PAIRS = SEGS // 2
@@ -341,7 +341,7 @@
     gathered = lax.all_to_all(outgoing.reshape(SEGS, ROWS, LANES), GATHER, 0, 0, tiled=True)
     held, rest, scale = make_replicas(sensor_positions, candidates, wavenumbers)
     messages = make_messages(sensor_order.reshape(SEGS, LANES), gathered, held, rest, scale)
-    received = lax.all_to_all(messages.reshape(PEERS, MSG // 2, 2, LANES), SPREAD, 0, 0, tiled=True)
+    received = lax.all_to_all(messages.reshape(PEERS, MSG, 1, LANES), SPREAD, 0, 0, tiled=True)
     return make_density(received.reshape(PEERS * MSG, LANES))
 
 

time: 65.9 us -> 65.5 us (level)
  no operation moved by 1% of the time
where the time goes in v4:
time: 65.5 us; the launch traced here: 65.2 us
  blocking collectives  33.9 us (52%)
  Pallas kernels  14.5 us (22%)
  starting transfers between devices  11.2 us (17%)
  waiting for transfers between devices  3.35 us (5%)
  local copies, waits for them, and re-layouts  1.58 us (2%)
  between operations  0.68 us (1%)
    all_to_all x1, blocking collectives, local(): lax.all_to_all(messages.reshape(PEERS, MSG, 1, LANES), SPREAD, 0, 0, tile...  33.9 us
    all_to_all x1, starting transfers between devices, local(): lax.all_to_all(outgoing.reshape(SEGS, ROWS, LANES), GATHER, 0, 0, tiled=T...  11.1 us
    pallas_call x1, Pallas kernels, make_replicas(): pl.pallas_call(replica_kernel, out_shape=(held, rest, jax.ShapeDtypeStruc...  7.46 us
    pallas_call x1, Pallas kernels, make_messages(): pl.pallas_call(message_kernel, out_shape=jax.ShapeDtypeStruct((PEERS * MS...  3.48 us
    all_to_all x1, waiting for transfers between devices, local(): lax.all_to_all(outgoing.reshape(SEGS, ROWS, LANES), GATHER, 0, 0, tiled=T...  2.82 us
    pallas_call x1, Pallas kernels, make_density(): pl.pallas_call(own_density_kernel, out_shape=(density, left, left, jax.Sh...  2.11 us
    broadcast_in_dim x1, local copies, waits for them, and re-layouts, local(): outgoing = jnp.broadcast_to(parts, (2, 2, 4, 2, ROWS, LANES))  1.57 us
    pallas_call x1, Pallas kernels, make_density(): pl.pallas_call(other_density_kernel, out_shape=density, in_specs=[in_vmem...  1.42 us
  transfers between devices with their start and end apart: 2, of which 2 were waited for; matrix products, arithmetic and copies ran while one was open for 0% of the time, Pallas kernels for 15%

profile of v4, /device:TPU:1, one launch (start us, length us, event | category | flops | bytes accessed | tf_op | source)
XLA Modules:
  0.0 65.2 jit_solution(9204478776331605950)
XLA Ops:
  0.6 0.0 copy-start
  0.6 1.6 %broadcast_in_dim.8 = f32[2,2,4,2,16,128]{5,4,3,2,1,0:T(8,128)} broadcast(f32[2,2,2,16,128]{4,3,2,1,0:T(8,128)} %bitcast.9), dimensions={0,1,3,4,5} | broadcast | bytes 327680 | tf_op jit(solution)/shard_map/broadcast_in_dim | solution.py:340
  2.2 11.1 %all-to-all-start = ((f32[32,16,128]{2,1,0:T(8,128)}), f32[32,16,128]{2,1,0:T(8,128)S(1)}, u32[]{:S(2)}, u32[]{:S(2)}) async-start(f32[32,16,128]{2,1,0:T(8,128)} %bitcast.2), calls=%async_computation | async-start | bytes 524288 | tf_op jit(solution)/shard_map/all_to_all | solution.py:341
  13.3 7.5 %replicas.1 = (bf16[6,2,256,512]{3,2,1,0:T(8,128)(2,1)S(1)}, bf16[10,2,256,512]{3,2,1,0:T(8,128)(2,1)}, f32[2,8,128]{2,1,0:T(8,128)S(1)}) custom-call(f32[2,4096]{1,0:T(2,128)} %pos_hbm.1, s32[4,1024]{1,0:T(4,128)} %cand_hbm.1, f32[4]{0:T(128)} %wave_hbm.1), custom_call_target="tpu_custom_call" | custom-call | flops 60000000 | bytes 10000000 | tf_op jit(solution)/shard_map/replicas/pallas_call | solution.py:157
  20.8 2.8 %all-to-all-done.spec_ref = f32[32,16,128]{2,1,0:T(8,128)S(1)} async-done(((f32[32,16,128]{2,1,0:T(8,128)}), f32[32,16,128]{2,1,0:T(8,128)S(1)}, u32[]{:S(2)}, u32[]{:S(2)}) %all-to-all-start) | async-done | bytes 262176 | tf_op jit(solution)/shard_map/all_to_all | solution.py:341
  23.6 0.0 copy-done
  23.6 3.5 %messages.1 = f32[3136,128]{1,0:T(8,128)S(1)} custom-call(s32[32,128]{1,0:T(8,128)S(1)} %bitcast.8, f32[32,16,128]{2,1,0:T(8,128)S(1)} %all-to-all-done.spec_ref, bf16[6,2,256,512]{3,2,1,0:T(8,128)(2,1)S(1)} %get-tuple-element.9.held_ref, bf16[10,2,256,512]{3,2,1,0:T(8,128)(2,1)} %get-tuple-element.10.rest_hbm, f32[2,8,128]{2,1,0:T(8,128)S(1)} %get-tuple-element.11.scale_ref), custom_call_target="tpu_custom_call" | custom-call | flops 100000000 | bytes 10000000 | tf_op jit(solution)/shard_map/messages/pallas_call | solution.py:222
  27.1 33.9 %all_to_all.10 = f32[64,49,1,128]{3,2,1,0:T(1,128)S(1)} all-to-all(f32[64,49,1,128]{3,2,1,0:T(1,128)S(1)} %bitcast.7), channel_id=1, replica_groups=mesh['xl'=2,'zh'=4,'zl'=2,'core'=2,'y'=4,'xh'=2] {'y','xl','xh','zl','co..., dimensions={0} | all-to-all | bytes 3211264 | tf_op jit(solution)/shard_map/all_to_all | solution.py:344
  61.0 0.1 columns.1
  61.0 0.1 collective-permute-start
  61.1 2.1 %own_density.1 = (f32[4,2,128,512]{3,2,1,0:T(8,128)}, bf16[4,256,256]{2,1,0:T(8,128)(2,1)S(1)}, bf16[4,256,256]{2,1,0:T(8,128)(2,1)S(1)}, f32[4,4]{1,0:T(4,128)}) custom-call(f32[3136,128]{1,0:T(8,128)S(1)} %bitcast.6), custom_call_target="tpu_custom_call" | custom-call | flops 800000000 | bytes 5000000 | tf_op jit(solution)/shard_map/own_density/pallas_call | solution.py:313
  63.3 0.5 collective-permute-done.got_ref
  63.8 1.4 %other_density.1 = f32[4,2,128,512]{3,2,1,0:T(8,128)} custom-call(bf16[4,256,256]{2,1,0:T(8,128)(2,1)S(1)} %get-tuple-element.12.high_ref, bf16[4,256,256]{2,1,0:T(8,128)(2,1)S(1)} %get-tuple-element.13.low_ref, f32[2048,128]{1,0:T(8,128)S(1)} %collective-permute-done.got_ref, ...), custom_call_target="tpu_custom_call", output_to_operand_aliasing={{}: (3, {})} | custom-call | flops 800000000 | bytes 5000000 | tf_op jit(solution)/shard_map/other_density/pallas_call | solution.py:324
Async XLA Ops:
  0.6 22.9 %copy-start = (s32[4096]{0:T(1024)S(1)}, s32[4096]{0:T(1024)}, u32[]{:S(2)}) copy-start(s32[4096]{0:T(1024)} %param.8) | copy-start | bytes 49156
  2.2 21.4 %all-to-all-start = ((f32[32,16,128]{2,1,0:T(8,128)}), f32[32,16,128]{2,1,0:T(8,128)S(1)}, u32[]{:S(2)}, u32[]{:S(2)}) async-start(f32[32,16,128]{2,1,0:T(8,128)} %bitcast.2), calls=%async_computation | async-start | bytes 524288 | tf_op jit(solution)/shard_map/all_to_all | solution.py:341
  61.0 2.7 %collective-permute-start = (f32[2048,128]{1,0:T(8,128)S(1)}, f32[2048,128]{1,0:T(8,128)S(1)}, u32[]{:S(2)}, u32[]{:S(2)}) collective-permute-start(f32[2048,128]{1,0:T(8,128)S(1)} %columns.1), channel_id=1, source_target_pairs={{0,8},{8,0},{1,9},{9,1},{2,10},{10,2},{3,11},{11,3},{4,12},{12,4},... | collective-permute-start | bytes 3145736 | tf_op jit(solution)/shard_map/ppermute | solution.py:323

commit v5 on v4

--- a/solution.py
+++ b/solution.py
@@ -249,12 +249,14 @@
 
 
 def send_out(freq, half, total, stage, out_ref, sem):
-    stage[freq, 0] = total[:LANES]
-    stage[freq, 1] = total[LANES:]
     columns = pl.ds(pl.multiple_of(half * 2 * LANES, 2 * LANES), 2 * LANES)
-    copy = pltpu.make_async_copy(stage.at[freq], out_ref.at[freq, :, :, columns], sem.at[freq])
-    copy.start()
-    return copy
+    copies = []
+    for part in range(2):
+        stage[freq, part] = total[part * LANES:(part + 1) * LANES]
+        copy = pltpu.make_async_copy(stage.at[freq, part], out_ref.at[freq, part, :, columns], sem.at[freq * 2 + part])
+        copy.start()
+        copies.append(copy)
+    return copies
 
 
 def column_kernel(got_ref, out_ref):
@@ -288,7 +290,7 @@
         high_ref[freq] = left_h
         low_ref[freq] = left_l
         total = product(left_h, left_l, got_ref, freq, ROWS)
-        copies.append(send_out(freq, lax.axis_index("core"), total, stage, out_ref, sem))
+        copies.extend(send_out(freq, lax.axis_index("core"), total, stage, out_ref, sem))
     for copy in copies:
         copy.wait()
 
@@ -298,7 +300,7 @@
     copies = []
     for freq in range(4):
         total = product(high_ref[freq], low_ref[freq], got_ref, freq, 0)
-        copies.append(send_out(freq, 1 - lax.axis_index("core"), total, stage, out_ref, sem))
+        copies.extend(send_out(freq, 1 - lax.axis_index("core"), total, stage, out_ref, sem))
     for copy in copies:
         copy.wait()
 
@@ -306,7 +308,7 @@
 def make_density(received):
     density = jax.ShapeDtypeStruct((4, 2, LANES, 4 * LANES), jnp.float32)
     left = jax.ShapeDtypeStruct((4, 2 * LANES, 2 * LANES), jnp.bfloat16)
-    scratch = [pltpu.VMEM((4, 2, LANES, 2 * LANES), jnp.float32), pltpu.SemaphoreType.DMA((4,))]
+    scratch = [pltpu.VMEM((4, 2, LANES, 2 * LANES), jnp.float32), pltpu.SemaphoreType.DMA((8,))]
     params = pltpu.CompilerParams(vmem_limit_bytes=VMEM_LIMIT)
     cost = pl.CostEstimate(flops=800_000_000, bytes_accessed=5_000_000, transcendentals=0)
     anywhere = in_hbm()

time: 65.5 us -> 65.5 us (level)
  no operation moved by 1% of the time
where the time goes in v5:
time: 65.5 us; the launch traced here: 65.2 us
  blocking collectives  33.9 us (52%)
  Pallas kernels  14.5 us (22%)
  starting transfers between devices  11.2 us (17%)
  waiting for transfers between devices  3.35 us (5%)
  local copies, waits for them, and re-layouts  1.58 us (2%)
  between operations  0.68 us (1%)
    all_to_all x1, blocking collectives, local(): lax.all_to_all(messages.reshape(PEERS, MSG, 1, LANES), SPREAD, 0, 0, tile...  33.9 us
    all_to_all x1, starting transfers between devices, local(): lax.all_to_all(outgoing.reshape(SEGS, ROWS, LANES), GATHER, 0, 0, tiled=T...  11.1 us
    pallas_call x1, Pallas kernels, make_replicas(): pl.pallas_call(replica_kernel, out_shape=(held, rest, jax.ShapeDtypeStruc...  7.46 us
    pallas_call x1, Pallas kernels, make_messages(): pl.pallas_call(message_kernel, out_shape=jax.ShapeDtypeStruct((PEERS * MS...  3.48 us
    all_to_all x1, waiting for transfers between devices, local(): lax.all_to_all(outgoing.reshape(SEGS, ROWS, LANES), GATHER, 0, 0, tiled=T...  2.82 us
    pallas_call x1, Pallas kernels, make_density(): pl.pallas_call(own_density_kernel, out_shape=(density, left, left, jax.Sh...  2.11 us
    broadcast_in_dim x1, local copies, waits for them, and re-layouts, local(): outgoing = jnp.broadcast_to(parts, (2, 2, 4, 2, ROWS, LANES))  1.57 us
    pallas_call x1, Pallas kernels, make_density(): pl.pallas_call(other_density_kernel, out_shape=density, in_specs=[in_vmem...  1.42 us
  transfers between devices with their start and end apart: 2, of which 2 were waited for; matrix products, arithmetic and copies ran while one was open for 0% of the time, Pallas kernels for 15%

profile of v5, /device:TPU:1, one launch (start us, length us, event | category | flops | bytes accessed | tf_op | source)
XLA Modules:
  0.0 65.2 jit_solution(16182878890468008079)
XLA Ops:
  0.6 0.0 copy-start
  0.6 1.6 %broadcast_in_dim.8 = f32[2,2,4,2,16,128]{5,4,3,2,1,0:T(8,128)} broadcast(f32[2,2,2,16,128]{4,3,2,1,0:T(8,128)} %bitcast.9), dimensions={0,1,3,4,5} | broadcast | bytes 327680 | tf_op jit(solution)/shard_map/broadcast_in_dim | solution.py:342
  2.2 11.1 %all-to-all-start = ((f32[32,16,128]{2,1,0:T(8,128)}), f32[32,16,128]{2,1,0:T(8,128)S(1)}, u32[]{:S(2)}, u32[]{:S(2)}) async-start(f32[32,16,128]{2,1,0:T(8,128)} %bitcast.2), calls=%async_computation | async-start | bytes 524288 | tf_op jit(solution)/shard_map/all_to_all | solution.py:343
  13.3 7.5 %replicas.1 = (bf16[6,2,256,512]{3,2,1,0:T(8,128)(2,1)S(1)}, bf16[10,2,256,512]{3,2,1,0:T(8,128)(2,1)}, f32[2,8,128]{2,1,0:T(8,128)S(1)}) custom-call(f32[2,4096]{1,0:T(2,128)} %pos_hbm.1, s32[4,1024]{1,0:T(4,128)} %cand_hbm.1, f32[4]{0:T(128)} %wave_hbm.1), custom_call_target="tpu_custom_call" | custom-call | flops 60000000 | bytes 10000000 | tf_op jit(solution)/shard_map/replicas/pallas_call | solution.py:157
  20.8 2.8 %all-to-all-done.spec_ref = f32[32,16,128]{2,1,0:T(8,128)S(1)} async-done(((f32[32,16,128]{2,1,0:T(8,128)}), f32[32,16,128]{2,1,0:T(8,128)S(1)}, u32[]{:S(2)}, u32[]{:S(2)}) %all-to-all-start) | async-done | bytes 262176 | tf_op jit(solution)/shard_map/all_to_all | solution.py:343
  23.6 0.0 copy-done
  23.6 3.5 %messages.1 = f32[3136,128]{1,0:T(8,128)S(1)} custom-call(s32[32,128]{1,0:T(8,128)S(1)} %bitcast.8, f32[32,16,128]{2,1,0:T(8,128)S(1)} %all-to-all-done.spec_ref, bf16[6,2,256,512]{3,2,1,0:T(8,128)(2,1)S(1)} %get-tuple-element.9.held_ref, bf16[10,2,256,512]{3,2,1,0:T(8,128)(2,1)} %get-tuple-element.10.rest_hbm, f32[2,8,128]{2,1,0:T(8,128)S(1)} %get-tuple-element.11.scale_ref), custom_call_target="tpu_custom_call" | custom-call | flops 100000000 | bytes 10000000 | tf_op jit(solution)/shard_map/messages/pallas_call | solution.py:222
  27.1 33.9 %all_to_all.10 = f32[64,49,1,128]{3,2,1,0:T(1,128)S(1)} all-to-all(f32[64,49,1,128]{3,2,1,0:T(1,128)S(1)} %bitcast.7), channel_id=1, replica_groups=mesh['xl'=2,'zh'=4,'zl'=2,'core'=2,'y'=4,'xh'=2] {'y','xl','xh','zl','co..., dimensions={0} | all-to-all | bytes 3211264 | tf_op jit(solution)/shard_map/all_to_all | solution.py:346
  61.0 0.1 columns.1
  61.0 0.1 collective-permute-start
  61.1 2.1 %own_density.1 = (f32[4,2,128,512]{3,2,1,0:T(8,128)}, bf16[4,256,256]{2,1,0:T(8,128)(2,1)S(1)}, bf16[4,256,256]{2,1,0:T(8,128)(2,1)S(1)}, f32[4,4]{1,0:T(4,128)}) custom-call(f32[3136,128]{1,0:T(8,128)S(1)} %bitcast.6), custom_call_target="tpu_custom_call" | custom-call | flops 800000000 | bytes 5000000 | tf_op jit(solution)/shard_map/own_density/pallas_call | solution.py:315
  63.3 0.5 collective-permute-done.got_ref
  63.8 1.4 %other_density.1 = f32[4,2,128,512]{3,2,1,0:T(8,128)} custom-call(bf16[4,256,256]{2,1,0:T(8,128)(2,1)S(1)} %get-tuple-element.12.high_ref, bf16[4,256,256]{2,1,0:T(8,128)(2,1)S(1)} %get-tuple-element.13.low_ref, f32[2048,128]{1,0:T(8,128)S(1)} %collective-permute-done.got_ref, ...), custom_call_target="tpu_custom_call", output_to_operand_aliasing={{}: (3, {})} | custom-call | flops 800000000 | bytes 5000000 | tf_op jit(solution)/shard_map/other_density/pallas_call | solution.py:326
Async XLA Ops:
  0.6 22.9 %copy-start = (s32[4096]{0:T(1024)S(1)}, s32[4096]{0:T(1024)}, u32[]{:S(2)}) copy-start(s32[4096]{0:T(1024)} %param.8) | copy-start | bytes 49156
  2.2 21.4 %all-to-all-start = ((f32[32,16,128]{2,1,0:T(8,128)}), f32[32,16,128]{2,1,0:T(8,128)S(1)}, u32[]{:S(2)}, u32[]{:S(2)}) async-start(f32[32,16,128]{2,1,0:T(8,128)} %bitcast.2), calls=%async_computation | async-start | bytes 524288 | tf_op jit(solution)/shard_map/all_to_all | solution.py:343
  61.0 2.7 %collective-permute-start = (f32[2048,128]{1,0:T(8,128)S(1)}, f32[2048,128]{1,0:T(8,128)S(1)}, u32[]{:S(2)}, u32[]{:S(2)}) collective-permute-start(f32[2048,128]{1,0:T(8,128)S(1)} %columns.1), channel_id=1, source_target_pairs={{0,8},{8,0},{1,9},{9,1},{2,10},{10,2},{3,11},{11,3},{4,12},{12,4},... | collective-permute-start | bytes 3145736 | tf_op jit(solution)/shard_map/ppermute | solution.py:325

commit v6 on v5

--- a/solution.py
+++ b/solution.py
@@ -251,9 +251,11 @@
 def send_out(freq, half, total, stage, out_ref, sem):
     columns = pl.ds(pl.multiple_of(half * 2 * LANES, 2 * LANES), 2 * LANES)
     copies = []
-    for part in range(2):
-        stage[freq, part] = total[part * LANES:(part + 1) * LANES]
-        copy = pltpu.make_async_copy(stage.at[freq, part], out_ref.at[freq, part, :, columns], sem.at[freq * 2 + part])
+    for piece in range(4):
+        part, rows = piece // 2, pl.ds(piece % 2 * 64, 64)
+        stage[freq, part, rows, :] = total[piece * 64:(piece + 1) * 64]
+        source, target = stage.at[freq, part, rows], out_ref.at[freq, part, rows, columns]
+        copy = pltpu.make_async_copy(source, target, sem.at[freq * 4 + piece])
         copy.start()
         copies.append(copy)
     return copies
@@ -308,7 +310,7 @@
 def make_density(received):
     density = jax.ShapeDtypeStruct((4, 2, LANES, 4 * LANES), jnp.float32)
     left = jax.ShapeDtypeStruct((4, 2 * LANES, 2 * LANES), jnp.bfloat16)
-    scratch = [pltpu.VMEM((4, 2, LANES, 2 * LANES), jnp.float32), pltpu.SemaphoreType.DMA((8,))]
+    scratch = [pltpu.VMEM((4, 2, LANES, 2 * LANES), jnp.float32), pltpu.SemaphoreType.DMA((16,))]
     params = pltpu.CompilerParams(vmem_limit_bytes=VMEM_LIMIT)
     cost = pl.CostEstimate(flops=800_000_000, bytes_accessed=5_000_000, transcendentals=0)
     anywhere = in_hbm()

time: 65.5 us -> 65.6 us (level)
  no operation moved by 1% of the time
where the time goes in v6:
time: 65.6 us; the launch traced here: 65.3 us
  blocking collectives  33.9 us (52%)
  Pallas kernels  14.6 us (22%)
  starting transfers between devices  11.2 us (17%)
  waiting for transfers between devices  3.3 us (5%)
  local copies, waits for them, and re-layouts  1.58 us (2%)
  between operations  0.68 us (1%)
    all_to_all x1, blocking collectives, local(): lax.all_to_all(messages.reshape(PEERS, MSG, 1, LANES), SPREAD, 0, 0, tile...  33.9 us
    all_to_all x1, starting transfers between devices, local(): lax.all_to_all(outgoing.reshape(SEGS, ROWS, LANES), GATHER, 0, 0, tiled=T...  11.1 us
    pallas_call x1, Pallas kernels, make_replicas(): pl.pallas_call(replica_kernel, out_shape=(held, rest, jax.ShapeDtypeStruc...  7.46 us
    pallas_call x1, Pallas kernels, make_messages(): pl.pallas_call(message_kernel, out_shape=jax.ShapeDtypeStruct((PEERS * MS...  3.48 us
    all_to_all x1, waiting for transfers between devices, local(): lax.all_to_all(outgoing.reshape(SEGS, ROWS, LANES), GATHER, 0, 0, tiled=T...  2.82 us
    pallas_call x1, Pallas kernels, make_density(): pl.pallas_call(own_density_kernel, out_shape=(density, left, left, jax.Sh...  2.16 us
    broadcast_in_dim x1, local copies, waits for them, and re-layouts, local(): outgoing = jnp.broadcast_to(parts, (2, 2, 4, 2, ROWS, LANES))  1.57 us
    pallas_call x1, Pallas kernels, make_density(): pl.pallas_call(other_density_kernel, out_shape=density, in_specs=[in_vmem...  1.47 us
  transfers between devices with their start and end apart: 2, of which 2 were waited for; matrix products, arithmetic and copies ran while one was open for 0% of the time, Pallas kernels for 15%

profile of v6, /device:TPU:1, one launch (start us, length us, event | category | flops | bytes accessed | tf_op | source)
XLA Modules:
  0.0 65.3 jit_solution(4503802672424205443)
XLA Ops:
  0.6 0.0 copy-start
  0.6 1.6 %broadcast_in_dim.8 = f32[2,2,4,2,16,128]{5,4,3,2,1,0:T(8,128)} broadcast(f32[2,2,2,16,128]{4,3,2,1,0:T(8,128)} %bitcast.9), dimensions={0,1,3,4,5} | broadcast | bytes 327680 | tf_op jit(solution)/shard_map/broadcast_in_dim | solution.py:344
  2.2 11.1 %all-to-all-start = ((f32[32,16,128]{2,1,0:T(8,128)}), f32[32,16,128]{2,1,0:T(8,128)S(1)}, u32[]{:S(2)}, u32[]{:S(2)}) async-start(f32[32,16,128]{2,1,0:T(8,128)} %bitcast.2), calls=%async_computation | async-start | bytes 524288 | tf_op jit(solution)/shard_map/all_to_all | solution.py:345
  13.3 7.5 %replicas.1 = (bf16[6,2,256,512]{3,2,1,0:T(8,128)(2,1)S(1)}, bf16[10,2,256,512]{3,2,1,0:T(8,128)(2,1)}, f32[2,8,128]{2,1,0:T(8,128)S(1)}) custom-call(f32[2,4096]{1,0:T(2,128)} %pos_hbm.1, s32[4,1024]{1,0:T(4,128)} %cand_hbm.1, f32[4]{0:T(128)} %wave_hbm.1), custom_call_target="tpu_custom_call" | custom-call | flops 60000000 | bytes 10000000 | tf_op jit(solution)/shard_map/replicas/pallas_call | solution.py:157
  20.8 2.8 %all-to-all-done.spec_ref = f32[32,16,128]{2,1,0:T(8,128)S(1)} async-done(((f32[32,16,128]{2,1,0:T(8,128)}), f32[32,16,128]{2,1,0:T(8,128)S(1)}, u32[]{:S(2)}, u32[]{:S(2)}) %all-to-all-start) | async-done | bytes 262176 | tf_op jit(solution)/shard_map/all_to_all | solution.py:345
  23.6 0.0 copy-done
  23.6 3.5 %messages.1 = f32[3136,128]{1,0:T(8,128)S(1)} custom-call(s32[32,128]{1,0:T(8,128)S(1)} %bitcast.8, f32[32,16,128]{2,1,0:T(8,128)S(1)} %all-to-all-done.spec_ref, bf16[6,2,256,512]{3,2,1,0:T(8,128)(2,1)S(1)} %get-tuple-element.9.held_ref, bf16[10,2,256,512]{3,2,1,0:T(8,128)(2,1)} %get-tuple-element.10.rest_hbm, f32[2,8,128]{2,1,0:T(8,128)S(1)} %get-tuple-element.11.scale_ref), custom_call_target="tpu_custom_call" | custom-call | flops 100000000 | bytes 10000000 | tf_op jit(solution)/shard_map/messages/pallas_call | solution.py:222
  27.1 33.9 %all_to_all.10 = f32[64,49,1,128]{3,2,1,0:T(1,128)S(1)} all-to-all(f32[64,49,1,128]{3,2,1,0:T(1,128)S(1)} %bitcast.7), channel_id=1, replica_groups=mesh['xl'=2,'zh'=4,'zl'=2,'core'=2,'y'=4,'xh'=2] {'y','xl','xh','zl','co..., dimensions={0} | all-to-all | bytes 3211264 | tf_op jit(solution)/shard_map/all_to_all | solution.py:348
  61.0 0.1 columns.1
  61.0 0.1 collective-permute-start
  61.1 2.2 %own_density.1 = (f32[4,2,128,512]{3,2,1,0:T(8,128)}, bf16[4,256,256]{2,1,0:T(8,128)(2,1)S(1)}, bf16[4,256,256]{2,1,0:T(8,128)(2,1)S(1)}, f32[4,4]{1,0:T(4,128)}) custom-call(f32[3136,128]{1,0:T(8,128)S(1)} %bitcast.6), custom_call_target="tpu_custom_call" | custom-call | flops 800000000 | bytes 5000000 | tf_op jit(solution)/shard_map/own_density/pallas_call | solution.py:317
  63.3 0.5 collective-permute-done.got_ref
  63.8 1.5 %other_density.1 = f32[4,2,128,512]{3,2,1,0:T(8,128)} custom-call(bf16[4,256,256]{2,1,0:T(8,128)(2,1)S(1)} %get-tuple-element.12.high_ref, bf16[4,256,256]{2,1,0:T(8,128)(2,1)S(1)} %get-tuple-element.13.low_ref, f32[2048,128]{1,0:T(8,128)S(1)} %collective-permute-done.got_ref, ...), custom_call_target="tpu_custom_call", output_to_operand_aliasing={{}: (3, {})} | custom-call | flops 800000000 | bytes 5000000 | tf_op jit(solution)/shard_map/other_density/pallas_call | solution.py:328
Async XLA Ops:
  0.6 22.9 %copy-start = (s32[4096]{0:T(1024)S(1)}, s32[4096]{0:T(1024)}, u32[]{:S(2)}) copy-start(s32[4096]{0:T(1024)} %param.8) | copy-start | bytes 49156
  2.2 21.4 %all-to-all-start = ((f32[32,16,128]{2,1,0:T(8,128)}), f32[32,16,128]{2,1,0:T(8,128)S(1)}, u32[]{:S(2)}, u32[]{:S(2)}) async-start(f32[32,16,128]{2,1,0:T(8,128)} %bitcast.2), calls=%async_computation | async-start | bytes 524288 | tf_op jit(solution)/shard_map/all_to_all | solution.py:345
  61.0 2.7 %collective-permute-start = (f32[2048,128]{1,0:T(8,128)S(1)}, f32[2048,128]{1,0:T(8,128)S(1)}, u32[]{:S(2)}, u32[]{:S(2)}) collective-permute-start(f32[2048,128]{1,0:T(8,128)S(1)} %columns.1), channel_id=1, source_target_pairs={{0,8},{8,0},{1,9},{9,1},{2,10},{10,2},{3,11},{11,3},{4,12},{12,4},... | collective-permute-start | bytes 3145736 | tf_op jit(solution)/shard_map/ppermute | solution.py:327
